TPU v7x, 512 devices: a whole 4x4x16 slice. The times are simulated.
512 devices in a mesh: tun: 128 (over z, x, core), hgt: 4 (over y).
Axes of the slice: x: 4, y: 4, z: 16, core: 2. Of those that a mesh axis runs over, the one named last changes fastest.
Arguments:
- cotangent: float32 [2, 512, 128, 256], P(None, 'tun', 'hgt'), may hold values from -16000 to 16000
- tun_cond: float32 [512, 128, 256], P('tun', 'hgt'), may hold values from 1024 to 2048
- tun_flow: float32 [512, 128, 256], P('tun', 'hgt'), may hold values from 32 to 64
- heat_loss: float32 [512, 128, 256], P('tun', 'hgt'), may hold values from 0.25 to 4
- hgt_cond: float32 [512, 128, 256], P('tun', 'hgt'), may hold values from 4096 to 16384
- hgt_lift: float32 [512, 128, 256], P('tun', 'hgt'), may hold values from 1024 to 4096
- wid_cond: float32 [257], replicated, may hold values from 0.25 to 1
Outputs:
- adjoint: float32 [2, 512, 128, 256], P(None, 'tun', 'hgt')
All inputs are finite; a program needn't handle non-finite values.
Results may differ from a plain program's by a relative error of at most 0.0049.
Values sent between devices are 32-bit elements; how exact they have to be, the bound alone decides.
No kernel may reach another device: no remote copies, remote signals or barrier semaphores. Data moves between devices by JAX's collectives and lax.ppermute only.
A program may use at most 192 MiB of HBM per device.

v0:
```python
import jax
import jax.numpy as jnp
from jax import lax
from jax.sharding import PartitionSpec as P


def passed_along(value, axis, steps):
    count = lax.axis_size(axis)
    first, last = (max(0, -steps), min(count, count - steps))
    return lax.ppermute(value, axis, [(source, source + steps) for source in range(first, last)])


def prefix_2(value, axis, join, neutral, backward):
    count, mine = (lax.axis_size(axis), lax.axis_index(axis))
    pieces = jax.tree.map(lambda part: lax.all_gather(part, axis), value)
    if backward:
        pieces = jax.tree.map(lambda part: part[::-1], pieces)
        mine = count - 1 - mine
    running = jax.tree.map(
        lambda part, zero: jnp.full_like(part, 0) + jnp.asarray(zero, part.dtype), value, neutral
    )

    def turn(position, running):
        longer = join(running, jax.tree.map(lambda part: part[position], pieces))
        return jax.tree.map(lambda new, old: jnp.where(position < mine, new, old), longer, running)

    return lax.fori_loop(0, count - 1, turn, running)


def pair_compose(earlier, latter):
    return (latter[0] + latter[1] * earlier[0], latter[1] * earlier[1])


def scaled(entries):
    largest = jnp.abs(entries[0])
    for member in entries[1:]:
        largest = jnp.maximum(largest, jnp.abs(member))
    return tuple((member / largest for member in entries))


def mobius_compose(earlier, latter):
    return scaled(
        tuple(
            (
                latter[2 * row_index] * earlier[col_index]
                + latter[2 * row_index + 1] * earlier[2 + col_index]
                for row_index in range(2)
                for col_index in range(2)
            )
        )
    )


def triple_compose(earlier, latter):
    return scaled(
        tuple(
            (
                latter[3 * row_index] * earlier[col_index]
                + latter[3 * row_index + 1] * earlier[3 + col_index]
                + latter[3 * row_index + 2] * earlier[6 + col_index]
                for row_index in range(3)
                for col_index in range(3)
            )
        )
    )


def matrix_identity(overall, matrix_order):
    zero_block = jnp.zeros_like(overall[0])
    ones_block = jnp.ones_like(overall[0])
    return tuple(
        (
            ones_block if row_index == col_index else zero_block
            for row_index in range(matrix_order)
            for col_index in range(matrix_order)
        )
    )


def pair_identity(overall):
    return (jnp.zeros_like(overall[0]), jnp.ones_like(overall[1]))


def local_front(overall):
    return matrix_identity(overall, 3)


def local_prefix(compose, members, chain_dim, reverse):
    moved = tuple((jnp.moveaxis(member, chain_dim, 0) for member in members))
    if reverse:
        start = tuple((member[-1] for member in moved))
        remaining = tuple((member[:-1] for member in moved))
    else:
        start = tuple((member[0] for member in moved))
        remaining = tuple((member[1:] for member in moved))

    def advance(accumulated, row_map):
        combined = compose(accumulated, row_map)
        return (combined, combined)

    unused, produced = lax.scan(advance, start, remaining, reverse=reverse)
    if reverse:
        joined = tuple(
            (jnp.concatenate([rows, first[None]], axis=0) for rows, first in zip(produced, start))
        )
    else:
        joined = tuple(
            (jnp.concatenate([first[None], rows], axis=0) for rows, first in zip(produced, start))
        )
    return tuple((jnp.moveaxis(member, 0, chain_dim) for member in joined))


def first_slice(values, chain_dim):
    return lax.index_in_dim(values, 0, chain_dim, keepdims=False)


def final_slice(values, chain_dim):
    return lax.index_in_dim(values, values.shape[chain_dim] - 1, chain_dim, keepdims=False)


def step_after(values, chain_dim, border):
    cell_count = values.shape[chain_dim]
    return jnp.concatenate(
        [
            lax.slice_in_dim(values, 1, cell_count, axis=chain_dim),
            jnp.expand_dims(border, chain_dim),
        ],
        axis=chain_dim,
    )


def transposed_rows(
    conduct, flow_face, added_diag, border_cond, border_flow, chain_dim, field_shape
):
    cond_next = step_after(conduct, chain_dim, border_cond)
    flow_next = step_after(flow_face, chain_dim, border_flow)
    main_diag = jnp.broadcast_to(1.0 + conduct + cond_next + flow_next + added_diag, field_shape)
    sub_diag = jnp.broadcast_to(-conduct, field_shape)
    super_diag = jnp.broadcast_to(-(cond_next + flow_next), field_shape)
    return (sub_diag, main_diag, super_diag)


def substitute_back(pivots, reduced, chain_dim, back_scan):
    suffix = local_prefix(pair_compose, (reduced, -pivots), chain_dim, True)
    incoming = back_scan((first_slice(suffix[0], chain_dim), first_slice(suffix[1], chain_dim)))
    return suffix[0] + suffix[1] * jnp.expand_dims(incoming[0], chain_dim)


def joint_solve(sub_diag, main_diag, super_diag, source, chain_dim, front_scan, back_scan):
    zero_block = jnp.zeros_like(main_diag)
    row_maps = (
        zero_block,
        zero_block,
        super_diag,
        zero_block,
        -sub_diag,
        source,
        -sub_diag,
        zero_block,
        main_diag,
    )
    prefix = local_prefix(triple_compose, row_maps, chain_dim, False)
    incoming = front_scan(tuple((final_slice(member, chain_dim) for member in prefix)))
    column = [jnp.expand_dims(incoming[position], chain_dim) for position in (2, 5, 8)]
    mapped = [
        prefix[3 * row_index] * column[0]
        + prefix[3 * row_index + 1] * column[1]
        + prefix[3 * row_index + 2] * column[2]
        for row_index in range(3)
    ]
    pivots = mapped[0] / mapped[2]
    reduced = mapped[1] / mapped[2]
    return substitute_back(pivots, reduced, chain_dim, back_scan)


def pivot_chain(sub_diag, main_diag, super_diag, chain_dim, front_scan):
    zero_block = jnp.zeros_like(main_diag)
    row_maps = (zero_block, super_diag, -sub_diag, main_diag)
    prefix = local_prefix(mobius_compose, row_maps, chain_dim, False)
    incoming = front_scan(tuple((final_slice(member, chain_dim) for member in prefix)))
    column = [jnp.expand_dims(incoming[1], chain_dim), jnp.expand_dims(incoming[3], chain_dim)]
    pivots = (prefix[0] * column[0] + prefix[1] * column[1]) / (
        prefix[2] * column[0] + prefix[3] * column[1]
    )
    entry_pivot = incoming[1] / incoming[3]
    return (pivots, entry_pivot)


def sweep_chain(sub_diag, main_diag, source, pivots, entry_pivot, chain_dim, sweep_scan):
    cell_count = pivots.shape[chain_dim]
    previous = jnp.concatenate(
        [
            jnp.expand_dims(entry_pivot, chain_dim),
            lax.slice_in_dim(pivots, 0, cell_count - 1, axis=chain_dim),
        ],
        axis=chain_dim,
    )
    denominator = main_diag - sub_diag * previous
    prefix = local_prefix(
        pair_compose, (source / denominator, -sub_diag / denominator), chain_dim, False
    )
    incoming = sweep_scan((final_slice(prefix[0], chain_dim), final_slice(prefix[1], chain_dim)))
    return prefix[0] + prefix[1] * jnp.expand_dims(incoming[0], chain_dim)


def per_device(cotangent, tun_cond, tun_flow, heat_loss, hgt_cond, hgt_lift, wid_cond):
    field_shape = cotangent.shape
    face_edge = passed_along(jnp.stack([tun_cond[0], tun_flow[0]]), "tun", -1)
    energy_loss = jnp.stack([heat_loss, jnp.zeros_like(heat_loss)])
    tunnel_rows = transposed_rows(
        tun_cond, tun_flow, energy_loss, face_edge[0], face_edge[1], 0, field_shape
    )

    def tunnel_back(overall):
        return prefix_2(overall, "tun", pair_compose, pair_identity(overall), True)

    def tunnel_pivots(overall):
        return prefix_2(overall, "tun", mobius_compose, matrix_identity(overall, 2), False)

    pivots, entry_pivot = pivot_chain(
        tunnel_rows[0], tunnel_rows[1], tunnel_rows[2], 1, tunnel_pivots
    )
    lift_pair = jnp.stack([hgt_cond, hgt_lift])
    local_field = lax.all_to_all(cotangent, "hgt", split_axis=1, concat_axis=2, tiled=True)
    local_coef = lax.all_to_all(lift_pair, "hgt", split_axis=1, concat_axis=2, tiled=True)
    zero_edge = jnp.zeros_like(local_coef[0][:, 0])
    height_rows = transposed_rows(
        local_coef[0], local_coef[1], 0.0, zero_edge, zero_edge, 1, local_field.shape
    )
    grouped = joint_solve(
        height_rows[0], height_rows[1], height_rows[2], local_field, 2, local_front, pair_identity
    )
    lifted = lax.all_to_all(grouped, "hgt", split_axis=2, concat_axis=1, tiled=True)

    def tunnel_sweep(overall):
        return prefix_2(overall, "tun", pair_compose, pair_identity(overall), False)

    reduced = sweep_chain(
        tunnel_rows[0], tunnel_rows[1], lifted, pivots, entry_pivot, 1, tunnel_sweep
    )
    carried = substitute_back(pivots, reduced, 1, tunnel_back)
    width_cells = wid_cond.shape[0] - 1
    main_width = 1.0 + wid_cond[:-1] + wid_cond[1:]
    off_width = -wid_cond[1:-1]
    zero_end = jnp.zeros((1,), jnp.float32)
    inverse = lax.linalg.tridiagonal_solve(
        jnp.concatenate([zero_end, off_width]),
        main_width,
        jnp.concatenate([off_width, zero_end]),
        jnp.eye(width_cells, dtype=jnp.float32),
    )
    flat = carried.reshape(-1, width_cells)
    solved = jnp.dot(flat, inverse, precision=lax.Precision.HIGHEST)
    return solved.reshape(field_shape)


def solution(mesh):
    in_specs = (
        P(None, "tun", "hgt", None),
        P("tun", "hgt", None),
        P("tun", "hgt", None),
        P("tun", "hgt", None),
        P("tun", "hgt", None),
        P("tun", "hgt", None),
        P(),
    )
    out_specs = P(None, "tun", "hgt", None)
    return jax.shard_map(
        per_device, mesh=mesh, in_specs=in_specs, out_specs=out_specs, check_vma=False
    )
```

profile of v0, /device:TPU:1, one launch (start us, length us, event | category | flops | bytes accessed | tf_op | source)
XLA Modules:
  0.0 2152.2 jit_solution(1086923241786016495)
XLA Ops:
  8.1 8.8 collective-permute-start
  18.7 1.6 add_add_fusion
  24.8 3.4 all-to-all-start
  29.8 5.4 all-to-all-done
  35.2 3.4 all-to-all-start.1
  38.8 5.9 all-to-all-done.1
  52.1 329.2 %while.212 = (s32[]{:T(128)}, f32[2,1,256]{2,1,0:T(1,128)S(1)}, f32[2,1,256]{2,1,0:T(1,128)S(1)}, f32[2,1,256]{2,1,0:T(1,128)S(1)}, f32[2,1,256]{2,1,0:T(1,128)S...) while((s32[]{:T(128)}, f32[2,1,256]{2,1,0:T(1,128)S(1)}, ...), condition=%wide.region_1.2_spmd.clone, body=%wide.region_0.1_spmd.clone.sunk | while | flops 35331 | bytes 120563 | solution.py:101
  382.0 2.2 fusion.39
  384.5 11.0 while.207
  396.4 3.4 all-to-all-start.2
  399.9 5.4 all-to-all-done.2
  405.5 56.7 %all-gather.21.cloned.1.call-done = f32[256,1,32,256]{3,2,1,0:T(8,128)} async-done(((f32[2,1,32,256]{3,2,1,0:T(8,128)}), f32[256,1,32,256]{3,2,1,0:T(8,128)}) %all-gather.21.cloned.1.call-update) | async-done | bytes 8388624 | tf_op jit(solution)/shard_map/all_gather | solution.py:15
  462.2 145.1 %all-gather.17.cloned.1.call-done = f32[256,1,32,256]{3,2,1,0:T(8,128)} async-done(((f32[2,1,32,256]{3,2,1,0:T(8,128)}), f32[256,1,32,256]{3,2,1,0:T(8,128)}) %all-gather.17.cloned.1.call-update) | async-done | bytes 8388624 | tf_op jit(solution)/shard_map/all_gather | solution.py:15
  607.3 137.7 %while.214 = (s32[]{:T(128)}, f32[2,32,256]{2,1,0:T(8,128)S(1)}, f32[2,32,256]{2,1,0:T(8,128)S(1)}, f32[2,32,256]{2,1,0:T(8,128)S(1)}, f32[2,32,256]{2,1,0:T(8,1...) while((s32[]{:T(128)}, f32[2,32,256]{2,1,0:T(8,128)S(1)}, ...), condition=%wide.region_7.8_spmd.clone, body=%wide.region_6.7_spmd.clone.sunk | while | flops 557060 | bytes 1507471 | solution.py:27
  608.4 1.0 divide_select_fusion.6
  609.5 1.0 divide_select_fusion.6
  610.5 1.0 divide_select_fusion.6
  612.7 1.0 divide_select_fusion.6
  613.8 1.0 divide_select_fusion.6
  614.9 1.0 divide_select_fusion.6
  616.0 1.0 divide_select_fusion.6
  617.0 1.0 divide_select_fusion.6
  745.2 1.0 divide_bitcast_fusion
  748.2 141.3 %all-gather.27.cloned.1.call-done = f32[256,1,32,256]{3,2,1,0:T(8,128)} async-done(((f32[2,1,32,256]{3,2,1,0:T(8,128)}), f32[256,1,32,256]{3,2,1,0:T(8,128)}) %all-gather.27.cloned.1.call-update) | async-done | bytes 8388624 | tf_op jit(solution)/shard_map/all_gather | solution.py:15
  889.4 145.0 %all-gather.25.cloned.1.call-done = f32[256,1,32,256]{3,2,1,0:T(8,128)} async-done(((f32[2,1,32,256]{3,2,1,0:T(8,128)}), f32[256,1,32,256]{3,2,1,0:T(8,128)}) %all-gather.25.cloned.1.call-update) | async-done | bytes 8388624 | tf_op jit(solution)/shard_map/all_gather | solution.py:15
  1034.5 119.0 %while.215 = (s32[]{:T(128)}, f32[2,32,256]{2,1,0:T(8,128)S(1)}, s32[]{:T(128)}, f32[128,2,32,256]{3,2,1,0:T(8,128)}, f32[128,2,32,256]{3,2,1,0:T(8,128)}, /*index=5*/s32[]{:T(128)}, s32[]{:T(128)}) while((s32[]{:T(128)}, f32[2,32,256]{2,1,0:T(8,128)S(1)}, s32[]{:T(128)}, f32[128,2,32,256]{3,2,1,0:T(8,128)}, ...), condition=%wide.region_11.12_spmd.clone, body=%wide.region_10.11_spmd.clone.sunk | while | flops 65540 | bytes 262245 | solution.py:27
  1160.1 593.8 %while.210 = (s32[]{:T(128)}, f32[]{:T(128)}, f32[256]{0:T(256)S(1)}, f32[7,32]{1,0:T(8,128)S(1)}, f32[7,32,256]{2,1,0:T(8,128)S(1)}, /*index=5*/f32[7,32]{1,0:T...) while((s32[]{:T(128)}, f32[]{:T(128)}, ...), condition=%wide.region_17.18_spmd, body=%wide.region_16.17_spmd.sunk | while | flops 24705 | bytes 269549 | solution.py:246
  1224.0 20.0 subtract_divide_fusion.125
  1308.8 20.0 subtract_divide_fusion.125
  1393.6 20.0 subtract_divide_fusion.125
  1478.5 20.0 subtract_divide_fusion.125
  1563.3 20.0 subtract_divide_fusion.125
  1648.1 20.0 subtract_divide_fusion.125
  1732.9 20.0 subtract_divide_fusion.125
  1813.0 19.5 subtract_divide_fusion.32
  1834.2 154.7 %while.211 = (s32[]{:T(128)}, f32[256]{0:T(256)S(1)}, f32[7,32,256]{2,1,0:T(8,128)S(1)}, f32[7,32,256]{2,1,0:T(8,128)S(1)}, f32[7,32]{1,0:T(8,128)S(1)}, /*index...) while((s32[]{:T(128)}, f32[256]{0:T(256)S(1)}, ...), condition=%wide.region_19.20_spmd, body=%wide.region_18.19_spmd.sunk | while | flops 16418 | bytes 266713 | solution.py:246
  1835.9 20.3 multiply_subtract_fusion.125
  1858.0 20.3 multiply_subtract_fusion.125
  1880.1 20.3 multiply_subtract_fusion.125
  1902.2 20.3 multiply_subtract_fusion.125
  1924.3 20.3 multiply_subtract_fusion.125
  1946.4 20.3 multiply_subtract_fusion.125
  1968.5 20.3 multiply_subtract_fusion.125
  1988.9 19.5 multiply_subtract_fusion.32
  2008.5 8.4 rev.7
  2016.9 8.4 rev.6
  2025.3 119.0 %while.216 = (s32[]{:T(128)}, f32[2,32,256]{2,1,0:T(8,128)S(1)}, s32[]{:T(128)}, f32[128,2,32,256]{3,2,1,0:T(8,128)}, f32[128,2,32,256]{3,2,1,0:T(8,128)}, /*index=5*/s32[]{:T(128)}, s32[]{:T(128)}) while((s32[]{:T(128)}, f32[2,32,256]{2,1,0:T(8,128)S(1)}, s32[]{:T(128)}, f32[128,2,32,256]{3,2,1,0:T(8,128)}, ...), condition=%wide.region_15.16_spmd.clone, body=%wide.region_14.15_spmd.clone.sunk | while | flops 65540 | bytes 262245 | solution.py:27
  2144.3 1.1 fusion.33
  (2243 shorter events, 767.1 us)
Async XLA Ops:
  6.5 17.6 copy-start.4
  6.5 17.6 copy-start.3
  6.5 21.8 %copy-start.2 = (f32[2,4,32,256]{3,2,1,0:T(8,128)S(1)}, f32[2,4,32,256]{3,2,1,0:T(8,128)}, u32[]{:S(2)}) copy-start(f32[2,4,32,256]{3,2,1,0:T(8,128)} %param.27) | copy-start | bytes 786436
  6.5 398.9 %all-gather.23.cloned.1.call-start = ((), (), s32[]{:S(2)}) async-start(), calls=%async_computation.6 | async-start | bytes 8454144 | tf_op jit(solution)/shard_map/all_gather | solution.py:15
  8.1 10.6 collective-permute-start
  22.6 382.9 %all-gather.19.cloned.1.call-start = ((), (), s32[]{:S(2)}) async-start(), calls=%async_computation.4 | async-start | bytes 8454144 | tf_op jit(solution)/shard_map/all_gather | solution.py:15
  23.4 438.8 %all-gather.21.cloned.1.call-start = ((), (), s32[]{:S(2)}) async-start(), calls=%async_computation.5 | async-start | bytes 8454144 | tf_op jit(solution)/shard_map/all_gather | solution.py:15
  24.8 10.3 all-to-all-start
  28.3 579.0 %all-gather.17.cloned.1.call-start = ((), (), s32[]{:S(2)}) async-start(), calls=%async_computation.3 | async-start | bytes 8454144 | tf_op jit(solution)/shard_map/all_gather | solution.py:15
  35.2 9.5 all-to-all-start.1
  52.1 693.1 %copy-start = (f32[4,32,256]{2,1,0:T(8,128)S(1)}, f32[4,32,256]{2,1,0:T(8,128)}, u32[]{:S(2)}) copy-start(f32[4,32,256]{2,1,0:T(8,128)} %param.28) | copy-start | bytes 393220
  381.3 0.7 copy-start.1
  396.4 9.0 all-to-all-start.2
  399.8 489.6 %all-gather.27.cloned.1.call-start = ((), (), s32[]{:S(2)}) async-start(), calls=%async_computation.8 | async-start | bytes 8454144 | tf_op jit(solution)/shard_map/all_gather | solution.py:15
  745.1 409.6 %copy-start.5 = (f32[257]{0:T(512)S(1)}, f32[257]{0:T(512)}, u32[]{:S(2)}) copy-start(f32[257]{0:T(512)} %param.33) | copy-start | bytes 3088
  747.2 287.2 %all-gather.25.cloned.1.call-start = ((), (), s32[]{:S(2)}) async-start(), calls=%async_computation.7 | async-start | bytes 8454144 | tf_op jit(solution)/shard_map/all_gather | solution.py:15
  748.0 1260.5 %all-gather.31.cloned.1.call-start = ((), (), s32[]{:S(2)}) async-start(), calls=%async_computation.10 | async-start | bytes 8454144 | tf_op jit(solution)/shard_map/all_gather | solution.py:15
  1154.5 862.4 %all-gather.29.cloned.1.call-start = ((), (), s32[]{:S(2)}) async-start(), calls=%async_computation.9 | async-start | bytes 8454144 | tf_op jit(solution)/shard_map/all_gather | solution.py:15
Sparse Core Ops, SparseCore 0:
  22.7 148.9 all-gather.22
  174.9 142.5 all-gather.18
  320.6 141.4 all-gather.20
  465.2 142.0 all-gather.16
  747.4 142.0 all-gather.26
  892.4 142.0 all-gather.24
  1154.6 142.7 all-gather.30
  1300.5 141.5 all-gather.28
where the time goes:
time: 2190 us; the launch traced here: 2150 us
  other arithmetic  799 us (36%)
  waiting for transfers between devices  505 us (23%)
  loops' own time  437 us (20%)
  local copies, waits for them, and re-layouts  317 us (14%)
  between operations  73.7 us (3%)
    all_gather x8, waiting for transfers between devices, prefix_2(): pieces = jax.tree.map(lambda part: lax.all_gather(part, axis), value)  488 us
    another operation x2, loops' own time, per_device(): lax.linalg.tridiagonal_solve(jnp.concatenate([zero_end, off_width]), main...  421 us
    select_n x508, other arithmetic, turn(): jnp.where(position < mine, new, old)  366 us
    dynamic_update_slice x762, local copies, waits for them, and re-layouts, local_prefix(): unused, produced = lax.scan(advance, start, remaining, reverse=reverse)  229 us
    sub x8, other arithmetic, per_device(): lax.linalg.tridiagonal_solve(jnp.concatenate([zero_end, off_width]), main...  161 us
    div x8, other arithmetic, per_device(): lax.linalg.tridiagonal_solve(jnp.concatenate([zero_end, off_width]), main...  160 us
    div x254, other arithmetic, scaled(): return tuple((member / largest for member in entries))  100 us
    slice x98, local copies, waits for them, and re-layouts, per_device(): lax.linalg.tridiagonal_solve(jnp.concatenate([zero_end, off_width]), main...  47.8 us
  transfers between devices with their start and end apart: 12, of which 7 were waited for; matrix products, arithmetic and copies ran while one was open for 34% of the time, Pallas kernels for 0%

commit v1 on v0

v1 whole, which is shorter than its diff:
```python
import jax
import jax.numpy as jnp
from jax import lax
from jax.experimental import pallas as pl
from jax.experimental.pallas import tpu as pltpu
from jax.sharding import PartitionSpec as P

F32 = jnp.float32
LANES = 128


def vmem(count):
    return [pl.BlockSpec(memory_space=pltpu.VMEM)] * count


def joined(element, following):
    up, mp, low, m, rp, r = element
    next_up, next_mp, next_low, next_m, next_rp, next_r = following
    mid = m + next_mp
    inverse = 1.0 / (mid + low + next_up)
    a, b, mid = low * inverse, next_up * inverse, mid * inverse
    c = [(one + two) * inverse for one, two in zip(r, next_rp)]
    whole = (
        up * b,
        mp + up * mid,
        next_low * a,
        next_m + next_low * mid,
        [one + up * two for one, two in zip(rp, c)],
        [one + next_low * two for one, two in zip(next_r, c)],
    )
    return whole, a, b, c


def height_forward(field, cond, lift, elements, saved, middle, pieces, fields, conds, lifts):
    lower = [pl.ds(0, 4, stride=2), pl.ds(1, 4, stride=2)]
    for half in range(2):
        lanes = pl.ds(half * LANES, LANES)

        fields[half], conds[half], lifts[half] = field[:, lanes], cond[:, lanes], lift[:, lanes]

        def cell(ref, index, base=0):
            return ref[half, pl.ds(base + index, 8, stride=16), :]

        def one(index):
            k = cell(conds, index)
            return (
                k + cell(lifts, index),
                jnp.zeros_like(k),
                k,
                jnp.ones_like(k),
                [jnp.zeros_like(k)] * 2,
                [cell(fields, index), cell(fields, index, 128)],
            )

        element = one(0)
        for index in range(1, 16):
            element, a, b, c = joined(element, one(index))
            for place, part in enumerate((a, b, *c)):
                saved[place, index - 1, :, lanes] = part
        up, mp, low, m, rp, r = element
        for place, part in enumerate((up, mp, low, m, *rp, *r)):
            pieces[half, place] = part

        def sub(which):
            up, mp, low, m, rp0, rp1, r0, r1 = (pieces[half, place, lower[which]] for place in range(8))
            return up, mp, low, m, [rp0, rp1], [r0, r1]

        whole, a, b, c = joined(sub(0), sub(1))
        for place, part in enumerate((a, b, *c)):
            middle[pl.ds(4 * place, 4), lanes] = part
        up, mp, low, m, rp, r = whole
        for place, part in enumerate((up, mp, low, m, *rp, *r)):
            for target in range(4):
                elements[target, pl.ds(4 * place, 4), lanes] = part


def height_back(elements, saved, middle, cond, flow, loss, sent, kept, bound, ends, lifted):
    def part(source, place, rows=4):
        return elements[source, pl.ds(4 * place, rows), :]

    rows_of = []
    for source in range(4):
        low, m, r = part(source, 2), part(source, 3), part(source, 6, 8)
        if source == 0:
            low, m = jnp.zeros_like(low), m + low
        up = jnp.zeros_like(low)
        if source < 3:
            up, m, r = part(source + 1, 0), m + part(source + 1, 1), r + part(source + 1, 4, 8)
        rows_of.append([low, m, up, r])

    def twice(value):
        return jnp.concatenate([value, value], axis=0)

    scale = []
    for source in range(4):
        low, m, up, r = rows_of[source]
        inverse = 1.0 / (m + up)
        scale.append((twice(up * inverse), r * twice(inverse)))
        if source < 3:
            after = rows_of[source + 1]
            after[1] = after[1] + after[0] * (m * inverse)
            after[3] = after[3] + twice(after[0]) * scale[source][1]
    bound[0] = jnp.zeros_like(bound[0])
    value = scale[3][1]
    bound[4] = value
    for source in (2, 1, 0):
        value = scale[source][1] + scale[source][0] * value
        bound[source + 1] = value
    mine = lax.axis_index("hgt")
    before, last = bound[mine], bound[mine + 1]
    a, b, c = middle[0:4, :], middle[4:8, :], middle[8:16, :]
    centre = c + twice(a) * before + twice(b) * last
    even, odd = pl.ds(0, 4, stride=2), pl.ds(1, 4, stride=2)
    for half in range(2):
        lanes = pl.ds(half * LANES, LANES)
        cut = slice(half * LANES, (half + 1) * LANES)
        for comp in range(2):
            rows = slice(4 * comp, 4 * comp + 4)
            ends[half, comp, 0, even] = before[rows, cut]
            ends[half, comp, 0, odd] = centre[rows, cut]
            ends[half, comp, 1, even] = centre[rows, cut]
            ends[half, comp, 1, odd] = last[rows, cut]
            start, value = ends[half, comp, 0], ends[half, comp, 1]
            lifted[half, pl.ds(128 * comp + 15, 8, stride=16), :] = value
            for index in range(14, -1, -1):
                value = (
                    saved[2 + comp, index, :, lanes]
                    + saved[0, index, :, lanes] * start
                    + saved[1, index, :, lanes] * value
                )
                lifted[half, pl.ds(128 * comp + index, 8, stride=16), :] = value
    for block in range(4):
        for half in range(2):
            lanes = pl.ds(half * LANES, LANES)
            for comp in range(2):

                def one(index):
                    rows = pl.ds(32 * index + 8 * block, 8)
                    k = cond[rows, lanes]
                    m = 1.0 + loss[rows, lanes] if comp == 0 else jnp.ones_like(k)
                    r = lifted[half, pl.ds(128 * comp + 32 * index + 8 * block, 8), :]
                    zero = jnp.zeros_like(k)
                    return k + flow[rows, lanes], zero, k, m, [zero], [r]

                element = one(0)
                for index in range(1, 4):
                    element, a, b, c = joined(element, one(index))
                    for place, value in enumerate((a, b, *c)):
                        kept[4 * comp + block, index - 1, place, :, lanes] = value
                up, mp, low, m, rp, r = element
                for place, value in enumerate((up, mp, low, m, *rp, *r)):
                    sent[4 * comp + block, place, :, lanes] = value


def chain_forward(received, sent, kept):
    def one(index):
        up, mp, low, m, rp, r = (received[index, place] for place in range(6))
        return up, mp, low, m, [rp], [r]

    element = one(0)
    for index in range(1, 8):
        element, a, b, c = joined(element, one(index))
        for place, value in enumerate((a, b, *c)):
            kept[index - 1, place] = value
    up, mp, low, m, rp, r = element
    for place, value in enumerate((up, mp, low, m, *rp, *r, *r, *r)):
        for half in range(2):
            sent[pl.ds(8 * half + place, 8, stride=16), :] = value[:, half * LANES : (half + 1) * LANES]


def chain_solve(received, sent):
    count = 16
    up, mp, low, m, rp, r = (received[pl.ds(place, count, stride=8), :] for place in range(6))

    def earlier(value, step):
        return jnp.concatenate([jnp.zeros_like(value[:step]), value[:-step]], axis=0)

    def later(value, step):
        return jnp.concatenate([value[step:], jnp.zeros_like(value[:step])], axis=0)

    first = lax.broadcasted_iota(jnp.int32, low.shape, 0) == 0
    m = m + later(mp, 1) + jnp.where(first, low, 0.0)
    low = jnp.where(first, 0.0, low)
    up, r = later(up, 1), r + later(rp, 1)
    step = 1
    while step < count:
        inverse = 1.0 / (low + m + up)
        part, right = m * inverse, r * inverse
        m, r, low, up = (
            m + low * earlier(part, step) + up * later(part, step),
            r + low * earlier(right, step) + up * later(right, step),
            low * earlier(low * inverse, step),
            up * later(up * inverse, step),
        )
        step *= 2
    value = r / m
    sent[pl.ds(0, count, stride=2), :] = earlier(value, 1)
    sent[pl.ds(1, count, stride=2), :] = value


def chain_back(received, kept, sent):
    def end(which):
        return jnp.concatenate([received[pl.ds(2 * half + which, 8, stride=4), :] for half in range(2)], axis=1)

    before, value = end(0), end(1)
    sent[7, 1] = value
    for index in range(6, -1, -1):
        value = kept[index, 2] + kept[index, 0] * before + kept[index, 1] * value
        sent[index, 1] = value
        sent[index + 1, 0] = value
    sent[0, 0] = before


def split(value):
    high = value.astype(jnp.bfloat16)
    return high, (value - high.astype(F32)).astype(jnp.bfloat16)


def tunnel_back(received, kept, high, low, out, carried):
    for group in range(8):
        comp, block = group // 4, group % 4
        before, value = received[group, 0], received[group, 1]
        for index in range(3, -1, -1):
            if index < 3:
                value = kept[group, index, 2] + kept[group, index, 0] * before + kept[group, index, 1] * value
            carried[pl.ds(128 * comp + 32 * index + 8 * block, 8), :] = value
    top, rest = split(carried[...])

    def times(one, two):
        return jnp.dot(one, two[...], preferred_element_type=F32)

    out[...] = times(top, high) + (times(top, low) + times(rest, high))


def width_inverse(below, above, high, low_part):
    count = 256
    step = 1
    lower, upper = below[...], above[...]
    row = lax.broadcasted_iota(jnp.int32, (count, LANES), 0)
    one = jnp.ones((count, LANES), F32)
    m = one + jnp.where(row == 0, lower, 0.0) + jnp.where(row == count - 1, upper, 0.0)
    low, up = jnp.where(row == 0, 0.0, lower), jnp.where(row == count - 1, 0.0, upper)
    column = lax.broadcasted_iota(jnp.int32, (count, LANES), 1)
    rights = [jnp.where(row == column + LANES * half, 1.0, 0.0) for half in range(2)]

    def earlier(value, step):
        return jnp.concatenate([jnp.zeros_like(value[:step]), value[:-step]], axis=0)

    def later(value, step):
        return jnp.concatenate([value[step:], jnp.zeros_like(value[:step])], axis=0)

    while step < count:
        inverse = 1.0 / (low + m + up)
        part = m * inverse
        scaled = [right * inverse for right in rights]
        rights = [
            right + low * earlier(value, step) + up * later(value, step) for right, value in zip(rights, scaled)
        ]
        m, low, up = (
            m + low * earlier(part, step) + up * later(part, step),
            low * earlier(low * inverse, step),
            up * later(up * inverse, step),
        )
        step *= 2
    for half in range(2):
        lanes = pl.ds(half * LANES, LANES)
        top, rest = split(rights[half] / m)
        high[:, lanes] = top
        low_part[:, lanes] = rest


def call(kernel, outs, scratch, *args):
    result = pl.pallas_call(
        kernel,
        out_shape=[jax.ShapeDtypeStruct(shape, dtype) for shape, dtype in outs],
        in_specs=vmem(len(args)),
        out_specs=vmem(len(outs)),
        scratch_shapes=[pltpu.VMEM(shape, F32) for shape in scratch],
        compiler_params=pltpu.CompilerParams(vmem_limit_bytes=16 * 2**20),
    )(*args)
    return result


def per_device(cotangent, tun_cond, tun_flow, heat_loss, hgt_cond, hgt_lift, wid_cond):
    near = [[8 * z + other for other in range(8)] for z in range(16)]
    far = [[8 * z + other for z in range(16)] for other in range(8)]

    def exchanged(value, axis, groups=None):
        return lax.all_to_all(value, axis, 0, 0, tiled=True, axis_index_groups=groups)

    def rows(value):
        return value.reshape(-1, 256)

    lower = jnp.broadcast_to(wid_cond[:256, None], (256, LANES))
    upper = jnp.broadcast_to(wid_cond[1:, None], (256, LANES))
    high, low = call(width_inverse, [((256, 256), jnp.bfloat16)] * 2, [], lower, upper)

    elements, saved, middle = call(
        height_forward,
        [((4, 32, 256), F32), ((4, 15, 8, 256), F32), ((16, 256), F32)],
        [(2, 8, 8, LANES), (2, 256, LANES), (2, 128, LANES), (2, 128, LANES)],
        rows(cotangent),
        rows(hgt_cond),
        rows(hgt_lift),
    )
    elements = exchanged(elements, "hgt")
    sent, kept = call(
        height_back,
        [((8, 6, 8, 256), F32), ((8, 3, 3, 8, 256), F32)],
        [(5, 8, 256), (2, 2, 2, 8, LANES), (2, 256, LANES)],
        elements,
        saved,
        middle,
        rows(tun_cond),
        rows(tun_flow),
        rows(heat_loss),
    )
    received = exchanged(sent, "tun", near)
    sent, chain = call(chain_forward, [((128, LANES), F32), ((7, 3, 8, 256), F32)], [], received)
    received = exchanged(sent.reshape(16, 8, LANES), "tun", far).reshape(128, LANES)
    [sent] = call(chain_solve, [((32, LANES), F32)], [], received)
    received = exchanged(sent.reshape(16, 2, LANES), "tun", far).reshape(32, LANES)
    [sent] = call(chain_back, [((8, 2, 8, 256), F32)], [], received, chain)
    received = exchanged(sent, "tun", near)
    [solved] = call(tunnel_back, [((256, 256), F32)], [(256, 256)], received, kept, high, low)
    return solved.reshape(cotangent.shape)


def solution(mesh):
    in_specs = (
        P(None, "tun", "hgt", None),
        P("tun", "hgt", None),
        P("tun", "hgt", None),
        P("tun", "hgt", None),
        P("tun", "hgt", None),
        P("tun", "hgt", None),
        P(),
    )
    out_specs = P(None, "tun", "hgt", None)
    return jax.shard_map(
        per_device, mesh=mesh, in_specs=in_specs, out_specs=out_specs, check_vma=False
    )
```

time: 2190 us -> 82.3 us (0.04); the launches traced: 2150 us -> 81.9 us
  other arithmetic: 799 us -> 0 us
  waiting for transfers between devices: 505 us -> 3.87 us
  loops' own time: 437 us -> 0 us
  local copies, waits for them, and re-layouts: 317 us -> 3.03 us
  between operations: 73.7 us -> 0.08 us
  blocking collectives: 0 us -> 64.6 us
    all_gather x8 -> x0, waiting for transfers between devices: 488 us -> none  [prefix_2(): pieces = jax.tree.map(lambda part: lax.all_gather(part, axis), value)]
    another operation x10 -> x0, loops' own time: 437 us -> none  [the longest x2 421 us: per_device(): lax.linalg.tridiagonal_solve(jnp.concatenate([zero_end, off_width]), main...]
    select_n x508 -> x0, other arithmetic: 366 us -> none  [turn(): jnp.where(position < mine, new, old)]
    div x263 -> x0, other arithmetic: 260 us -> none  [the longest x8 160 us: per_device(): lax.linalg.tridiagonal_solve(jnp.concatenate([zero_end, off_width]), main...]
    dynamic_update_slice x783 -> x0, local copies, waits for them, and re-layouts: 230 us -> none  [the longest x762 229 us: local_prefix(): unused, produced = lax.scan(advance, start, remaining, reverse=reverse)]
    sub x8 -> x0, other arithmetic: 161 us -> none  [per_device(): lax.linalg.tridiagonal_solve(jnp.concatenate([zero_end, off_width]), main...]
    all_to_all x0 -> x4, blocking collectives: none -> 64.6 us  [exchanged(): lax.all_to_all(value, axis, 0, 0, tiled=True, axis_index_groups=groups)]
    slice x136 -> x1, local copies, waits for them, and re-layouts: 57.2 us -> 0.07 us  [per_device(): upper = jnp.broadcast_to(wid_cond[1:, None], (256, LANES))]
  transfers between devices with their start and end apart: 12 -> 1, of which waited for: 7 -> 1; matrix products, arithmetic and copies ran while one was open for 34% -> 0% of each run, Pallas kernels for 0% -> 1%
where the time goes in v1:
time: 82.3 us; the launch traced here: 81.9 us
  blocking collectives  64.6 us (78%)
  starting transfers between devices  6.78 us (8%)
  waiting for transfers between devices  3.87 us (5%)
  Pallas kernels  3.53 us (4%)
  local copies, waits for them, and re-layouts  3.03 us (4%)
    all_to_all x4, blocking collectives, exchanged(): lax.all_to_all(value, axis, 0, 0, tiled=True, axis_index_groups=groups)  64.6 us
    all_to_all x1, starting transfers between devices, exchanged(): lax.all_to_all(value, axis, 0, 0, tiled=True, axis_index_groups=groups)  6.78 us
    all_to_all x1, waiting for transfers between devices, exchanged(): lax.all_to_all(value, axis, 0, 0, tiled=True, axis_index_groups=groups)  3.87 us
    pallas_call x7, Pallas kernels, call(): pl.pallas_call(kernel, out_shape=[jax.ShapeDtypeStruct(shape, dtype) for...  3.53 us
    unnamed x14, local copies, waits for them, and re-layouts  2.78 us
  transfers between devices with their start and end apart: 1, of which 1 were waited for; matrix products, arithmetic and copies ran while one was open for 0% of the time, Pallas kernels for 1%

profile of v1, /device:TPU:1, one launch (start us, length us, event | category | flops | bytes accessed | tf_op | source)
XLA Modules:
  0.0 81.9 jit_solution(15773446736111168278)
XLA Ops:
  0.0 0.0 copy-start
  0.0 0.9 %copy-done = f32[2,4,32,256]{3,2,1,0:T(8,128)S(1)} copy-done((f32[2,4,32,256]{3,2,1,0:T(8,128)S(1)}, f32[2,4,32,256]{3,2,1,0:T(8,128)}, u32[]{:S(2)}) %copy-start) | copy-done | bytes 262168
  1.0 0.0 copy-start.1
  1.0 0.9 %copy-done.1 = f32[4,32,256]{2,1,0:T(8,128)S(1)} copy-done((f32[4,32,256]{2,1,0:T(8,128)S(1)}, f32[4,32,256]{2,1,0:T(8,128)}, u32[]{:S(2)}) %copy-start.1) | copy-done | bytes 131096
  1.9 0.0 copy-start.2
  1.9 0.9 %copy-done.2 = f32[4,32,256]{2,1,0:T(8,128)S(1)} copy-done((f32[4,32,256]{2,1,0:T(8,128)S(1)}, f32[4,32,256]{2,1,0:T(8,128)}, u32[]{:S(2)}) %copy-start.2) | copy-done | bytes 131096
  2.8 0.0 copy-start.5
  2.8 0.3 shard_map.73
  3.1 0.0 copy-start.3
  3.1 0.0 copy-start.4
  3.1 9.8 %all_to_all.25.elements = f32[4,32,256]{2,1,0:T(8,128)S(1)} all-to-all(f32[4,32,256]{2,1,0:T(8,128)S(1)} %get-tuple-element.14), channel_id=1, replica_groups=mesh['tun'=128,'hgt'=4] {'hgt'}, dimensions={0} | all-to-all | bytes 262144 | tf_op jit(solution)/shard_map/all_to_all | solution.py:289
  12.9 0.0 copy-done.5
  12.9 0.0 copy-done.3
  12.9 0.0 copy-done.4
  12.9 0.3 shard_map.74
  13.1 16.1 %all_to_all.26.received = f32[8,6,8,256]{3,2,1,0:T(8,128)S(1)} all-to-all(f32[8,6,8,256]{3,2,1,0:T(8,128)S(1)} %get-tuple-element.17), channel_id=1, replica_groups={{0,4,8,12,16,20,24,28},{32,36,40,44,48,52,56,60},{64,68,72,76,80,84,88,..., dimensions={0} | all-to-all | bytes 786432 | tf_op jit(solution)/shard_map/all_to_all | solution.py:289
  29.2 0.1 shard_map.75
  29.3 24.5 %all_to_all.27 = f32[16,8,128]{2,1,0:T(8,128)S(1)} all-to-all(f32[16,8,128]{2,1,0:T(8,128)S(1)} %bitcast.20), channel_id=1, replica_groups={{0,32,64,96,128,160,192,224,256,288,320,352,384,416,448,480},{4,36,68,1..., dimensions={0} | all-to-all | bytes 131072 | tf_op jit(solution)/shard_map/all_to_all | solution.py:289
  53.8 0.1 shard_map.76
  53.9 14.3 %all_to_all.28 = f32[16,2,128]{2,1,0:T(2,128)S(1)} all-to-all(f32[16,2,128]{2,1,0:T(2,128)S(1)} %bitcast.19), channel_id=1, replica_groups={{0,32,64,96,128,160,192,224,256,288,320,352,384,416,448,480},{4,36,68,1..., dimensions={0} | all-to-all | bytes 32768 | tf_op jit(solution)/shard_map/all_to_all | solution.py:289
  68.2 0.7 shard_map.77
  68.8 0.0 copy-start.6
  68.9 6.8 %all-to-all-start.4 = ((f32[8,2,8,256]{3,2,1,0:T(8,128)}), f32[8,2,8,256]{3,2,1,0:T(8,128)S(1)}, u32[]{:S(2)}, u32[]{:S(2)}) async-start(f32[8,2,8,256]{3,2,1,0:T(8,128)} %shard_map.77), calls=%async_computation.4 | async-start | bytes 262144 | tf_op jit(solution)/shard_map/all_to_all | solution.py:289
  75.6 0.0 copy-done.6
  75.6 0.1 fusion
  75.7 0.1 broadcast_in_dim.4.below
  75.8 0.1 broadcast_in_dim.5.above
  75.9 1.1 %shard_map.78 = (bf16[256,256]{1,0:T(8,128)(2,1)S(1)}, bf16[256,256]{1,0:T(8,128)(2,1)S(1)}) custom-call(f32[256,128]{1,0:T(8,128)S(1)} %broadcast_in_dim.4.below, f32[256,128]{1,0:T(8,128)S(1)} %broadcast_in_dim.5.above), custom_call_target="tpu_custom_call" | custom-call | tf_op jit(solution)/shard_map/pallas_call | solution.py:273
  77.1 3.9 %all-to-all-done.4.received = f32[8,2,8,256]{3,2,1,0:T(8,128)S(1)} async-done(((f32[8,2,8,256]{3,2,1,0:T(8,128)}), f32[8,2,8,256]{3,2,1,0:T(8,128)S(1)}, u32[]{:S(2)}, u32[]{:S(2)}) %all-to-all-start.4) | async-done | bytes 131104 | tf_op jit(solution)/shard_map/all_to_all | solution.py:289
  80.9 1.0 %shard_map.79 = f32[256,256]{1,0:T(8,128)} custom-call(f32[8,2,8,256]{3,2,1,0:T(8,128)S(1)} %all-to-all-done.4.received, f32[8,3,3,8,256]{4,3,2,1,0:T(8,128)S(1)} %get-tuple-element.20.kept, bf16[256,256]{1,0:T(8,128)(2,1)S(1)} %get-tuple-element.21.high, bf16[256,256]{1,0:T(8,128)(2,1)S(1)} %get-tuple-element.22.low), custom_call_target="tpu_custom_call" | custom-call | tf_op jit(solution)/shard_map/pallas_call | solution.py:273
Async XLA Ops:
  0.0 0.9 %copy-start = (f32[2,4,32,256]{3,2,1,0:T(8,128)S(1)}, f32[2,4,32,256]{3,2,1,0:T(8,128)}, u32[]{:S(2)}) copy-start(f32[2,4,32,256]{3,2,1,0:T(8,128)} %param.7) | copy-start | bytes 786436
  1.0 0.9 %copy-start.1 = (f32[4,32,256]{2,1,0:T(8,128)S(1)}, f32[4,32,256]{2,1,0:T(8,128)}, u32[]{:S(2)}) copy-start(f32[4,32,256]{2,1,0:T(8,128)} %param.11) | copy-start | bytes 393220
  1.9 0.9 %copy-start.2 = (f32[4,32,256]{2,1,0:T(8,128)S(1)}, f32[4,32,256]{2,1,0:T(8,128)}, u32[]{:S(2)}) copy-start(f32[4,32,256]{2,1,0:T(8,128)} %param.12) | copy-start | bytes 393220
  2.8 10.1 %copy-start.5 = (f32[4,32,256]{2,1,0:T(8,128)S(1)}, f32[4,32,256]{2,1,0:T(8,128)}, u32[]{:S(2)}) copy-start(f32[4,32,256]{2,1,0:T(8,128)} %param.10) | copy-start | bytes 393220
  3.1 9.8 %copy-start.3 = (f32[4,32,256]{2,1,0:T(8,128)S(1)}, f32[4,32,256]{2,1,0:T(8,128)}, u32[]{:S(2)}) copy-start(f32[4,32,256]{2,1,0:T(8,128)} %param.8) | copy-start | bytes 393220
  3.1 9.8 %copy-start.4 = (f32[4,32,256]{2,1,0:T(8,128)S(1)}, f32[4,32,256]{2,1,0:T(8,128)}, u32[]{:S(2)}) copy-start(f32[4,32,256]{2,1,0:T(8,128)} %param.9) | copy-start | bytes 393220
  68.8 6.8 %copy-start.6 = (f32[257]{0:T(512)S(1)}, f32[257]{0:T(512)}, u32[]{:S(2)}) copy-start(f32[257]{0:T(512)} %param.13) | copy-start | bytes 3088
  68.9 12.1 %all-to-all-start.4 = ((f32[8,2,8,256]{3,2,1,0:T(8,128)}), f32[8,2,8,256]{3,2,1,0:T(8,128)S(1)}, u32[]{:S(2)}, u32[]{:S(2)}) async-start(f32[8,2,8,256]{3,2,1,0:T(8,128)} %shard_map.77), calls=%async_computation.4 | async-start | bytes 262144 | tf_op jit(solution)/shard_map/all_to_all | solution.py:289

commit v2 on v1

--- a/solution.py
+++ b/solution.py
@@ -149,7 +149,28 @@
                         kept[4 * comp + block, index - 1, place, :, lanes] = value
                 up, mp, low, m, rp, r = element
                 for place, value in enumerate((up, mp, low, m, *rp, *r)):
-                    sent[4 * comp + block, place, :, lanes] = value
+                    sent[2 * (4 * comp + block) + half, place] = value
+
+
+def tree(elements, first, last, keep):
+    if last - first == 1:
+        return elements(first)
+    centre = (first + last) // 2
+    left, right = tree(elements, first, centre, keep), tree(elements, centre, last, keep)
+    whole, a, b, c = joined(left, right)
+    keep(centre - 1, a, b, c)
+    return whole
+
+
+def untree(kept, first, last, before, value, give):
+    if last - first == 1:
+        return
+    centre = (first + last) // 2
+    a, b, c = kept(centre - 1)
+    middle = c + a * before + b * value
+    give(centre - 1, middle)
+    untree(kept, first, centre, before, middle, give)
+    untree(kept, centre, last, middle, value, give)
 
 
 def chain_forward(received, sent, kept):
@@ -157,58 +178,46 @@
         up, mp, low, m, rp, r = (received[index, place] for place in range(6))
         return up, mp, low, m, [rp], [r]
 
-    element = one(0)
-    for index in range(1, 8):
-        element, a, b, c = joined(element, one(index))
-        for place, value in enumerate((a, b, *c)):
-            kept[index - 1, place] = value
-    up, mp, low, m, rp, r = element
-    for place, value in enumerate((up, mp, low, m, *rp, *r, *r, *r)):
-        for half in range(2):
-            sent[pl.ds(8 * half + place, 8, stride=16), :] = value[:, half * LANES : (half + 1) * LANES]
-
-
-def chain_solve(received, sent):
-    count = 16
-    up, mp, low, m, rp, r = (received[pl.ds(place, count, stride=8), :] for place in range(6))
-
-    def earlier(value, step):
-        return jnp.concatenate([jnp.zeros_like(value[:step]), value[:-step]], axis=0)
-
-    def later(value, step):
-        return jnp.concatenate([value[step:], jnp.zeros_like(value[:step])], axis=0)
-
-    first = lax.broadcasted_iota(jnp.int32, low.shape, 0) == 0
-    m = m + later(mp, 1) + jnp.where(first, low, 0.0)
-    low = jnp.where(first, 0.0, low)
-    up, r = later(up, 1), r + later(rp, 1)
-    step = 1
-    while step < count:
-        inverse = 1.0 / (low + m + up)
-        part, right = m * inverse, r * inverse
-        m, r, low, up = (
-            m + low * earlier(part, step) + up * later(part, step),
-            r + low * earlier(right, step) + up * later(right, step),
-            low * earlier(low * inverse, step),
-            up * later(up * inverse, step),
-        )
-        step *= 2
-    value = r / m
-    sent[pl.ds(0, count, stride=2), :] = earlier(value, 1)
-    sent[pl.ds(1, count, stride=2), :] = value
-
-
-def chain_back(received, kept, sent):
-    def end(which):
-        return jnp.concatenate([received[pl.ds(2 * half + which, 8, stride=4), :] for half in range(2)], axis=1)
-
-    before, value = end(0), end(1)
-    sent[7, 1] = value
-    for index in range(6, -1, -1):
-        value = kept[index, 2] + kept[index, 0] * before + kept[index, 1] * value
+    def keep(index, a, b, c):
+        kept[index, 0], kept[index, 1], kept[index, 2] = a, b, c[0]
+
+    up, mp, low, m, rp, r = tree(one, 0, received.shape[0], keep)
+    for place, value in enumerate((up, mp, low, m, *rp, *r)):
+        for target in range(sent.shape[0]):
+            sent[target, place] = value
+
+
+def chain_back(received, kept, sent, bound):
+    groups, members = received.shape[0], sent.shape[0]
+    top = {}
+
+    def one(index):
+        up, mp, low, m, rp, r = (received[index, place] for place in range(6))
+        return up, mp, low, m, [rp], [r]
+
+    def keep(index, a, b, c):
+        top[index] = a, b, c[0]
+
+    def give(index, value):
+        bound[index + 1] = value
+
+    up, mp, low, m, rp, r = tree(one, 0, groups, keep)
+    zero = jnp.zeros_like(up)
+    value = r[0] / (low + m)
+    bound[0] = zero
+    give(groups - 1, value)
+    untree(lambda index: top[index], 0, groups, zero, value, give)
+    mine = lax.axis_index("tun") // members
+    before, value = bound[mine], bound[mine + 1]
+
+    def end(index, value):
         sent[index, 1] = value
-        sent[index + 1, 0] = value
+        if index + 1 < members:
+            sent[index + 1, 0] = value
+
     sent[0, 0] = before
+    end(members - 1, value)
+    untree(lambda index: [kept[index, place] for place in range(3)], 0, members, before, value, end)
 
 
 def split(value):
@@ -219,11 +228,14 @@
 def tunnel_back(received, kept, high, low, out, carried):
     for group in range(8):
         comp, block = group // 4, group % 4
-        before, value = received[group, 0], received[group, 1]
-        for index in range(3, -1, -1):
-            if index < 3:
-                value = kept[group, index, 2] + kept[group, index, 0] * before + kept[group, index, 1] * value
-            carried[pl.ds(128 * comp + 32 * index + 8 * block, 8), :] = value
+        for half in range(2):
+            lanes = pl.ds(half * LANES, LANES)
+            before, value = received[2 * group + half, 0], received[2 * group + half, 1]
+            for index in range(3, -1, -1):
+                if index < 3:
+                    a, b, c = (kept[group, index, place, :, lanes] for place in range(3))
+                    value = c + a * before + b * value
+                carried[pl.ds(128 * comp + 32 * index + 8 * block, 8), lanes] = value
     top, rest = split(carried[...])
 
     def times(one, two):
@@ -282,8 +294,11 @@
 
 
 def per_device(cotangent, tun_cond, tun_flow, heat_loss, hgt_cond, hgt_lift, wid_cond):
-    near = [[8 * z + other for other in range(8)] for z in range(16)]
-    far = [[8 * z + other for z in range(16)] for other in range(8)]
+    members = 16
+    count = lax.axis_size("tun")
+    near = [list(range(first, first + members)) for first in range(0, count, members)]
+    far = [list(range(first, count, members)) for first in range(members)]
+    groups = len(near)
 
     def exchanged(value, axis, groups=None):
         return lax.all_to_all(value, axis, 0, 0, tiled=True, axis_index_groups=groups)
@@ -306,7 +321,7 @@
     elements = exchanged(elements, "hgt")
     sent, kept = call(
         height_back,
-        [((8, 6, 8, 256), F32), ((8, 3, 3, 8, 256), F32)],
+        [((members, 6, 8, LANES), F32), ((8, 3, 3, 8, 256), F32)],
         [(5, 8, 256), (2, 2, 2, 8, LANES), (2, 256, LANES)],
         elements,
         saved,
@@ -316,11 +331,13 @@
         rows(heat_loss),
     )
     received = exchanged(sent, "tun", near)
-    sent, chain = call(chain_forward, [((128, LANES), F32), ((7, 3, 8, 256), F32)], [], received)
-    received = exchanged(sent.reshape(16, 8, LANES), "tun", far).reshape(128, LANES)
-    [sent] = call(chain_solve, [((32, LANES), F32)], [], received)
-    received = exchanged(sent.reshape(16, 2, LANES), "tun", far).reshape(32, LANES)
-    [sent] = call(chain_back, [((8, 2, 8, 256), F32)], [], received, chain)
+    sent, chain = call(
+        chain_forward, [((groups, 6, 8, LANES), F32), ((members - 1, 3, 8, LANES), F32)], [], received
+    )
+    received = exchanged(sent, "tun", far)
+    [sent] = call(
+        chain_back, [((members, 2, 8, LANES), F32)], [(groups + 1, 8, LANES)], received, chain
+    )
     received = exchanged(sent, "tun", near)
     [solved] = call(tunnel_back, [((256, 256), F32)], [(256, 256)], received, kept, high, low)
     return solved.reshape(cotangent.shape)

time: 82.3 us -> 74.3 us (0.903)
  blocking collectives: 64.6 us -> 54.3 us
  starting transfers between devices: 6.78 us -> 8.31 us
  waiting for transfers between devices: 3.87 us -> 4.8 us
    all_to_all x4 -> x3, blocking collectives: 64.6 us -> 54.3 us  [exchanged(): lax.all_to_all(value, axis, 0, 0, tiled=True, axis_index_groups=groups)]
    all_to_all x1, starting transfers between devices: 6.78 us -> 8.31 us  [exchanged(): lax.all_to_all(value, axis, 0, 0, tiled=True, axis_index_groups=groups)]
    all_to_all x1, waiting for transfers between devices: 3.87 us -> 4.8 us  [exchanged(): lax.all_to_all(value, axis, 0, 0, tiled=True, axis_index_groups=groups)]
    pallas_call x7 -> x6, Pallas kernels: 3.53 us -> 3.49 us  [call(): pl.pallas_call(kernel, out_shape=[jax.ShapeDtypeStruct(shape, dtype) for...]
  transfers between devices with their start and end apart: 1 -> 1, of which waited for: 1 -> 1; matrix products, arithmetic and copies ran while one was open for 0% -> 0% of each run, Pallas kernels for 1% -> 2%
where the time goes in v2:
time: 74.3 us; the launch traced here: 74 us
  blocking collectives  54.3 us (73%)
  starting transfers between devices  8.31 us (11%)
  waiting for transfers between devices  4.8 us (6%)
  Pallas kernels  3.49 us (5%)
  local copies, waits for them, and re-layouts  3.03 us (4%)
    all_to_all x3, blocking collectives, exchanged(): lax.all_to_all(value, axis, 0, 0, tiled=True, axis_index_groups=groups)  54.3 us
    all_to_all x1, starting transfers between devices, exchanged(): lax.all_to_all(value, axis, 0, 0, tiled=True, axis_index_groups=groups)  8.31 us
    all_to_all x1, waiting for transfers between devices, exchanged(): lax.all_to_all(value, axis, 0, 0, tiled=True, axis_index_groups=groups)  4.8 us
    pallas_call x6, Pallas kernels, call(): pl.pallas_call(kernel, out_shape=[jax.ShapeDtypeStruct(shape, dtype) for...  3.49 us
    unnamed x14, local copies, waits for them, and re-layouts  2.78 us
  transfers between devices with their start and end apart: 1, of which 1 were waited for; matrix products, arithmetic and copies ran while one was open for 0% of the time, Pallas kernels for 2%

profile of v2, /device:TPU:1, one launch (start us, length us, event | category | flops | bytes accessed | tf_op | source)
XLA Modules:
  0.0 74.0 jit_solution(1563624526916275873)
XLA Ops:
  0.0 0.0 copy-start
  0.0 0.9 %copy-done = f32[2,4,32,256]{3,2,1,0:T(8,128)S(1)} copy-done((f32[2,4,32,256]{3,2,1,0:T(8,128)S(1)}, f32[2,4,32,256]{3,2,1,0:T(8,128)}, u32[]{:S(2)}) %copy-start) | copy-done | bytes 262168
  1.0 0.0 copy-start.1
  1.0 0.9 %copy-done.1 = f32[4,32,256]{2,1,0:T(8,128)S(1)} copy-done((f32[4,32,256]{2,1,0:T(8,128)S(1)}, f32[4,32,256]{2,1,0:T(8,128)}, u32[]{:S(2)}) %copy-start.1) | copy-done | bytes 131096
  1.9 0.0 copy-start.2
  1.9 0.9 %copy-done.2 = f32[4,32,256]{2,1,0:T(8,128)S(1)} copy-done((f32[4,32,256]{2,1,0:T(8,128)S(1)}, f32[4,32,256]{2,1,0:T(8,128)}, u32[]{:S(2)}) %copy-start.2) | copy-done | bytes 131096
  2.8 0.0 copy-start.5
  2.8 0.3 shard_map.73
  3.1 0.0 copy-start.3
  3.1 0.0 copy-start.4
  3.1 9.8 %all_to_all.20.elements = f32[4,32,256]{2,1,0:T(8,128)S(1)} all-to-all(f32[4,32,256]{2,1,0:T(8,128)S(1)} %get-tuple-element.14), channel_id=1, replica_groups=mesh['tun'=128,'hgt'=4] {'hgt'}, dimensions={0} | all-to-all | bytes 262144 | tf_op jit(solution)/shard_map/all_to_all | solution.py:304
  12.9 0.0 copy-done.5
  12.9 0.0 copy-done.3
  12.9 0.0 copy-done.4
  12.9 0.3 shard_map.74
  13.1 16.5 %all_to_all.21.received = f32[16,6,8,128]{3,2,1,0:T(8,128)S(1)} all-to-all(f32[16,6,8,128]{3,2,1,0:T(8,128)S(1)} %get-tuple-element.17), channel_id=1, replica_groups={{0,4,8,12,16,20,24,28,32,36,40,44,48,52,56,60},{64,68,72,76,80,84,88,92..., dimensions={0} | all-to-all | bytes 786432 | tf_op jit(solution)/shard_map/all_to_all | solution.py:304
  29.6 0.1 shard_map.75
  29.7 28.0 %all_to_all.22.received = f32[8,6,8,128]{3,2,1,0:T(8,128)S(1)} all-to-all(f32[8,6,8,128]{3,2,1,0:T(8,128)S(1)} %get-tuple-element.18), channel_id=1, replica_groups={{0,64,128,192,256,320,384,448},{4,68,132,196,260,324,388,452},{8,72,136..., dimensions={0} | all-to-all | bytes 393216 | tf_op jit(solution)/shard_map/all_to_all | solution.py:304
  57.7 0.7 shard_map.76
  58.5 0.0 copy-start.6
  58.5 8.3 %all-to-all-start.3 = ((f32[16,2,8,128]{3,2,1,0:T(8,128)}), f32[16,2,8,128]{3,2,1,0:T(8,128)S(1)}, u32[]{:S(2)}, u32[]{:S(2)}) async-start(f32[16,2,8,128]{3,2,1,0:T(8,128)} %shard_map.76), calls=%async_computation.3 | async-start | bytes 262144 | tf_op jit(solution)/shard_map/all_to_all | solution.py:304
  66.8 0.0 copy-done.6
  66.8 0.1 fusion
  66.9 0.1 broadcast_in_dim.4.below
  67.0 0.1 broadcast_in_dim.5.above
  67.1 1.1 %shard_map.77 = (bf16[256,256]{1,0:T(8,128)(2,1)S(1)}, bf16[256,256]{1,0:T(8,128)(2,1)S(1)}) custom-call(f32[256,128]{1,0:T(8,128)S(1)} %broadcast_in_dim.4.below, f32[256,128]{1,0:T(8,128)S(1)} %broadcast_in_dim.5.above), custom_call_target="tpu_custom_call" | custom-call | tf_op jit(solution)/shard_map/pallas_call | solution.py:285
  68.2 4.8 %all-to-all-done.3.received = f32[16,2,8,128]{3,2,1,0:T(8,128)S(1)} async-done(((f32[16,2,8,128]{3,2,1,0:T(8,128)}), f32[16,2,8,128]{3,2,1,0:T(8,128)S(1)}, u32[]{:S(2)}, u32[]{:S(2)}) %all-to-all-start.3) | async-done | bytes 131104 | tf_op jit(solution)/shard_map/all_to_all | solution.py:304
  73.0 1.0 %shard_map.78 = f32[256,256]{1,0:T(8,128)} custom-call(f32[16,2,8,128]{3,2,1,0:T(8,128)S(1)} %all-to-all-done.3.received, f32[8,3,3,8,256]{4,3,2,1,0:T(8,128)S(1)} %get-tuple-element.20.kept, bf16[256,256]{1,0:T(8,128)(2,1)S(1)} %get-tuple-element.21.high, bf16[256,256]{1,0:T(8,128)(2,1)S(1)} %get-tuple-element.22.low), custom_call_target="tpu_custom_call" | custom-call | tf_op jit(solution)/shard_map/pallas_call | solution.py:285
Async XLA Ops:
  0.0 0.9 %copy-start = (f32[2,4,32,256]{3,2,1,0:T(8,128)S(1)}, f32[2,4,32,256]{3,2,1,0:T(8,128)}, u32[]{:S(2)}) copy-start(f32[2,4,32,256]{3,2,1,0:T(8,128)} %param.7) | copy-start | bytes 786436
  1.0 0.9 %copy-start.1 = (f32[4,32,256]{2,1,0:T(8,128)S(1)}, f32[4,32,256]{2,1,0:T(8,128)}, u32[]{:S(2)}) copy-start(f32[4,32,256]{2,1,0:T(8,128)} %param.11) | copy-start | bytes 393220
  1.9 0.9 %copy-start.2 = (f32[4,32,256]{2,1,0:T(8,128)S(1)}, f32[4,32,256]{2,1,0:T(8,128)}, u32[]{:S(2)}) copy-start(f32[4,32,256]{2,1,0:T(8,128)} %param.12) | copy-start | bytes 393220
  2.8 10.1 %copy-start.5 = (f32[4,32,256]{2,1,0:T(8,128)S(1)}, f32[4,32,256]{2,1,0:T(8,128)}, u32[]{:S(2)}) copy-start(f32[4,32,256]{2,1,0:T(8,128)} %param.10) | copy-start | bytes 393220
  3.1 9.8 %copy-start.3 = (f32[4,32,256]{2,1,0:T(8,128)S(1)}, f32[4,32,256]{2,1,0:T(8,128)}, u32[]{:S(2)}) copy-start(f32[4,32,256]{2,1,0:T(8,128)} %param.8) | copy-start | bytes 393220
  3.1 9.8 %copy-start.4 = (f32[4,32,256]{2,1,0:T(8,128)S(1)}, f32[4,32,256]{2,1,0:T(8,128)}, u32[]{:S(2)}) copy-start(f32[4,32,256]{2,1,0:T(8,128)} %param.9) | copy-start | bytes 393220
  58.5 8.3 %copy-start.6 = (f32[257]{0:T(512)S(1)}, f32[257]{0:T(512)}, u32[]{:S(2)}) copy-start(f32[257]{0:T(512)} %param.13) | copy-start | bytes 3088
  58.5 14.5 %all-to-all-start.3 = ((f32[16,2,8,128]{3,2,1,0:T(8,128)}), f32[16,2,8,128]{3,2,1,0:T(8,128)S(1)}, u32[]{:S(2)}, u32[]{:S(2)}) async-start(f32[16,2,8,128]{3,2,1,0:T(8,128)} %shard_map.76), calls=%async_computation.3 | async-start | bytes 262144 | tf_op jit(solution)/shard_map/all_to_all | solution.py:304

commit v3 on v2

--- a/solution.py
+++ b/solution.py
@@ -7,10 +7,6 @@
 
 F32 = jnp.float32
 LANES = 128
-
-
-def vmem(count):
-    return [pl.BlockSpec(memory_space=pltpu.VMEM)] * count
 
 
 def joined(element, following):
@@ -31,12 +27,29 @@
     return whole, a, b, c
 
 
-def height_forward(field, cond, lift, elements, saved, middle, pieces, fields, conds, lifts):
+def front(field, cond, lift, wide, elements, saved, middle, high, rest, pieces, fields, conds, lifts, face, done):
+    face_copy = pltpu.make_async_copy(wide, face, done.at[6])
+    face_copy.start()
+    copies = []
+    for source, target in ((field, fields), (cond, conds), (lift, lifts)):
+        for half in range(2):
+            copy = pltpu.make_async_copy(
+                source.at[:, pl.ds(half * LANES, LANES)], target.at[half], done.at[len(copies)]
+            )
+            copy.start()
+            copies.append(copy)
+    face_copy.wait()
+    width_inverse(face, high, rest)
+    for copy in copies:
+        copy.wait()
+    height_forward(elements, saved, middle, pieces, fields, conds, lifts)
+
+
+def height_forward(elements, saved, middle, pieces, fields, conds, lifts):
     lower = [pl.ds(0, 4, stride=2), pl.ds(1, 4, stride=2)]
     for half in range(2):
         lanes = pl.ds(half * LANES, LANES)
 
-        fields[half], conds[half], lifts[half] = field[:, lanes], cond[:, lanes], lift[:, lanes]
 
         def cell(ref, index, base=0):
             return ref[half, pl.ds(base + index, 8, stride=16), :]
@@ -225,7 +238,7 @@
     return high, (value - high.astype(F32)).astype(jnp.bfloat16)
 
 
-def tunnel_back(received, kept, high, low, out, carried):
+def tunnel_back(received, kept, high, low, out, carried, solved, done):
     for group in range(8):
         comp, block = group // 4, group % 4
         for half in range(2):
@@ -236,18 +249,31 @@
                     a, b, c = (kept[group, index, place, :, lanes] for place in range(3))
                     value = c + a * before + b * value
                 carried[pl.ds(128 * comp + 32 * index + 8 * block, 8), lanes] = value
-    top, rest = split(carried[...])
 
     def times(one, two):
         return jnp.dot(one, two[...], preferred_element_type=F32)
 
-    out[...] = times(top, high) + (times(top, low) + times(rest, high))
-
-
-def width_inverse(below, above, high, low_part):
+    copies = []
+    for part in range(4):
+        rows = pl.ds(64 * part, 64)
+        top, rest = split(carried[rows, :])
+        solved[rows, :] = times(top, high) + (times(top, low) + times(rest, high))
+        copy = pltpu.make_async_copy(solved.at[rows, :], out.at[rows, :], done.at[part])
+        copy.start()
+        copies.append(copy)
+    for copy in copies:
+        copy.wait()
+
+
+def width_inverse(face, high, low_part):
     count = 256
     step = 1
-    lower, upper = below[...], above[...]
+
+    def filled(start):
+        parts = [face[start + LANES * half : start + LANES * (half + 1)] for half in range(2)]
+        return jnp.concatenate([jnp.transpose(jnp.broadcast_to(part.reshape(1, LANES), (LANES, LANES))) for part in parts], axis=0)
+
+    lower, upper = filled(0), filled(1)
     row = lax.broadcasted_iota(jnp.int32, (count, LANES), 0)
     one = jnp.ones((count, LANES), F32)
     m = one + jnp.where(row == 0, lower, 0.0) + jnp.where(row == count - 1, upper, 0.0)
@@ -281,16 +307,21 @@
         low_part[:, lanes] = rest
 
 
-def call(kernel, outs, scratch, *args):
-    result = pl.pallas_call(
+def call(kernel, outs, scratch, *args, place=pltpu.VMEM, out_place=pltpu.VMEM):
+    if place is pltpu.HBM:
+        args = [pltpu.with_memory_space_constraint(arg, place) for arg in args]
+    return pl.pallas_call(
         kernel,
         out_shape=[jax.ShapeDtypeStruct(shape, dtype) for shape, dtype in outs],
-        in_specs=vmem(len(args)),
-        out_specs=vmem(len(outs)),
-        scratch_shapes=[pltpu.VMEM(shape, F32) for shape in scratch],
+        in_specs=[pl.BlockSpec(memory_space=place)] * len(args),
+        out_specs=[pl.BlockSpec(memory_space=out_place)] * len(outs),
+        scratch_shapes=scratch,
         compiler_params=pltpu.CompilerParams(vmem_limit_bytes=16 * 2**20),
     )(*args)
-    return result
+
+
+def room(*shape):
+    return pltpu.VMEM(shape, F32)
 
 
 def per_device(cotangent, tun_cond, tun_flow, heat_loss, hgt_cond, hgt_lift, wid_cond):
@@ -306,23 +337,28 @@
     def rows(value):
         return value.reshape(-1, 256)
 
-    lower = jnp.broadcast_to(wid_cond[:256, None], (256, LANES))
-    upper = jnp.broadcast_to(wid_cond[1:, None], (256, LANES))
-    high, low = call(width_inverse, [((256, 256), jnp.bfloat16)] * 2, [], lower, upper)
-
-    elements, saved, middle = call(
-        height_forward,
-        [((4, 32, 256), F32), ((4, 15, 8, 256), F32), ((16, 256), F32)],
-        [(2, 8, 8, LANES), (2, 256, LANES), (2, 128, LANES), (2, 128, LANES)],
+    elements, saved, middle, high, low = call(
+        front,
+        [((4, 32, 256), F32), ((4, 15, 8, 256), F32), ((16, 256), F32), *[((256, 256), jnp.bfloat16)] * 2],
+        [
+            room(2, 8, 8, LANES),
+            room(2, 256, LANES),
+            room(2, 128, LANES),
+            room(2, 128, LANES),
+            room(257),
+            pltpu.SemaphoreType.DMA((7,)),
+        ],
         rows(cotangent),
         rows(hgt_cond),
         rows(hgt_lift),
+        wid_cond,
+        place=pltpu.HBM,
     )
     elements = exchanged(elements, "hgt")
     sent, kept = call(
         height_back,
         [((members, 6, 8, LANES), F32), ((8, 3, 3, 8, 256), F32)],
-        [(5, 8, 256), (2, 2, 2, 8, LANES), (2, 256, LANES)],
+        [room(5, 8, 256), room(2, 2, 2, 8, LANES), room(2, 256, LANES)],
         elements,
         saved,
         middle,
@@ -336,10 +372,19 @@
     )
     received = exchanged(sent, "tun", far)
     [sent] = call(
-        chain_back, [((members, 2, 8, LANES), F32)], [(groups + 1, 8, LANES)], received, chain
+        chain_back, [((members, 2, 8, LANES), F32)], [room(groups + 1, 8, LANES)], received, chain
     )
     received = exchanged(sent, "tun", near)
-    [solved] = call(tunnel_back, [((256, 256), F32)], [(256, 256)], received, kept, high, low)
+    [solved] = call(
+        tunnel_back,
+        [((256, 256), F32)],
+        [room(256, 256), room(256, 256), pltpu.SemaphoreType.DMA((4,))],
+        received,
+        kept,
+        high,
+        low,
+        out_place=pltpu.HBM,
+    )
     return solved.reshape(cotangent.shape)
 
 

time: 74.3 us -> 72.4 us (0.974)
  blocking collectives: 54.3 us -> 68.2 us
  starting transfers between devices: 8.31 us -> 0 us
  waiting for transfers between devices: 4.8 us -> 0 us
  local copies, waits for them, and re-layouts: 3.03 us -> 0.02 us
    all_to_all x3 -> x4, blocking collectives: 54.3 us -> 68.2 us  [exchanged(): lax.all_to_all(value, axis, 0, 0, tiled=True, axis_index_groups=groups)]
    all_to_all x1 -> x0, starting transfers between devices: 8.31 us -> none  [exchanged(): lax.all_to_all(value, axis, 0, 0, tiled=True, axis_index_groups=groups)]
    all_to_all x1 -> x0, waiting for transfers between devices: 4.8 us -> none  [exchanged(): lax.all_to_all(value, axis, 0, 0, tiled=True, axis_index_groups=groups)]
    unnamed x14 -> x6, local copies, waits for them, and re-layouts: 2.78 us -> 0.02 us
    pallas_call x6 -> x5, Pallas kernels: 3.49 us -> 3.9 us  [call(): pl.pallas_call(kernel, out_shape=[jax.ShapeDtypeStruct(shape, dtype) for...]
  transfers between devices with their start and end apart: 1 -> 0, of which waited for: 1 -> 0; matrix products, arithmetic and copies ran while one was open for 0% -> 0% of each run, Pallas kernels for 2% -> 0%
where the time goes in v3:
time: 72.4 us; the launch traced here: 72.2 us
  blocking collectives  68.2 us (94%)
  Pallas kernels  3.9 us (5%)
    all_to_all x4, blocking collectives, exchanged(): lax.all_to_all(value, axis, 0, 0, tiled=True, axis_index_groups=groups)  68.2 us
    pallas_call x5, Pallas kernels, call(): pl.pallas_call(kernel, out_shape=[jax.ShapeDtypeStruct(shape, dtype) for...  3.9 us

profile of v3, /device:TPU:1, one launch (start us, length us, event | category | flops | bytes accessed | tf_op | source)
XLA Modules:
  0.0 72.2 jit_solution(12484899503182170381)
XLA Ops:
  0.0 0.0 copy-start.2
  0.0 2.4 %shard_map.73 = (f32[4,32,256]{2,1,0:T(8,128)S(1)}, f32[4,15,8,256]{3,2,1,0:T(8,128)S(1)}, f32[16,256]{1,0:T(8,128)S(1)}, bf16[256,256]{1,0:T(8,128)(2,1)S(1)}, bf16[256,256]{1,0:T(8,128)(2,1)S(1)}) custom-call(f32[256,256]{1,0:T(8,128)} %bitcast.10, f32[128,256]{1,0:T(8,128)} %bitcast.11, f32[128,256]{1,0:T(8,128)} %bitcast.12, f32[257]{0:T(512)} %wide.1), custom_call_target="tpu_custom_call" | custom-call | tf_op jit(solution)/shard_map/pallas_call | solution.py:313
  2.4 0.0 copy-start
  2.4 0.0 copy-start.1
  2.5 9.8 %all_to_all.20.elements = f32[4,32,256]{2,1,0:T(8,128)S(1)} all-to-all(f32[4,32,256]{2,1,0:T(8,128)S(1)} %get-tuple-element.14), channel_id=1, replica_groups=mesh['tun'=128,'hgt'=4] {'hgt'}, dimensions={0} | all-to-all | bytes 262144 | tf_op jit(solution)/shard_map/all_to_all | solution.py:335
  12.2 0.0 copy-done.2
  12.2 0.0 copy-done
  12.2 0.0 copy-done.1
  12.2 0.3 shard_map.74
  12.5 16.5 %all_to_all.21.received = f32[16,6,8,128]{3,2,1,0:T(8,128)S(1)} all-to-all(f32[16,6,8,128]{3,2,1,0:T(8,128)S(1)} %get-tuple-element.17), channel_id=1, replica_groups={{0,4,8,12,16,20,24,28,32,36,40,44,48,52,56,60},{64,68,72,76,80,84,88,92..., dimensions={0} | all-to-all | bytes 786432 | tf_op jit(solution)/shard_map/all_to_all | solution.py:335
  29.0 0.1 shard_map.75
  29.1 28.0 %all_to_all.22.received = f32[8,6,8,128]{3,2,1,0:T(8,128)S(1)} all-to-all(f32[8,6,8,128]{3,2,1,0:T(8,128)S(1)} %get-tuple-element.18), channel_id=1, replica_groups={{0,64,128,192,256,320,384,448},{4,68,132,196,260,324,388,452},{8,72,136..., dimensions={0} | all-to-all | bytes 393216 | tf_op jit(solution)/shard_map/all_to_all | solution.py:335
  57.1 0.1 shard_map.76
  57.2 13.9 %all_to_all.23.received = f32[16,2,8,128]{3,2,1,0:T(8,128)S(1)} all-to-all(f32[16,2,8,128]{3,2,1,0:T(8,128)S(1)} %shard_map.76), channel_id=1, replica_groups={{0,4,8,12,16,20,24,28,32,36,40,44,48,52,56,60},{64,68,72,76,80,84,88,92..., dimensions={0} | all-to-all | bytes 262144 | tf_op jit(solution)/shard_map/all_to_all | solution.py:335
  71.1 1.1 %shard_map.77 = f32[256,256]{1,0:T(8,128)} custom-call(f32[16,2,8,128]{3,2,1,0:T(8,128)S(1)} %all_to_all.23.received, f32[8,3,3,8,256]{4,3,2,1,0:T(8,128)S(1)} %get-tuple-element.20.kept, bf16[256,256]{1,0:T(8,128)(2,1)S(1)} %get-tuple-element.21.high, bf16[256,256]{1,0:T(8,128)(2,1)S(1)} %get-tuple-element.22.low), custom_call_target="tpu_custom_call" | custom-call | tf_op jit(solution)/shard_map/pallas_call | solution.py:313
Async XLA Ops:
  0.0 12.2 %copy-start.2 = (f32[4,32,256]{2,1,0:T(8,128)S(1)}, f32[4,32,256]{2,1,0:T(8,128)}, u32[]{:S(2)}) copy-start(f32[4,32,256]{2,1,0:T(8,128)} %param.10) | copy-start | bytes 393220
  2.4 9.8 %copy-start = (f32[4,32,256]{2,1,0:T(8,128)S(1)}, f32[4,32,256]{2,1,0:T(8,128)}, u32[]{:S(2)}) copy-start(f32[4,32,256]{2,1,0:T(8,128)} %param.8) | copy-start | bytes 393220
  2.4 9.8 %copy-start.1 = (f32[4,32,256]{2,1,0:T(8,128)S(1)}, f32[4,32,256]{2,1,0:T(8,128)}, u32[]{:S(2)}) copy-start(f32[4,32,256]{2,1,0:T(8,128)} %param.9) | copy-start | bytes 393220

commit v4 on v3

--- a/solution.py
+++ b/solution.py
@@ -7,6 +7,15 @@
 
 F32 = jnp.float32
 LANES = 128
+
+HEIGHT_ORDER = (2, 3, 0, 1)
+JOIN_ORDER = (4, 5, 6, 7, 8, 9, 10, 11, 12, 13, 14, 15, 0, 1, 2, 3)
+FAR_ORDER = (5, 6, 7, 0, 1, 2, 3, 4)
+BACK_ORDER = (4, 5, 6, 7, 8, 9, 10, 11, 12, 13, 14, 15, 0, 1, 2, 3)
+
+
+def places(order):
+    return [order.index(member) for member in range(len(order))]
 
 
 def joined(element, following):
@@ -89,9 +98,9 @@
 
 def height_back(elements, saved, middle, cond, flow, loss, sent, kept, bound, ends, lifted):
     def part(source, place, rows=4):
-        return elements[source, pl.ds(4 * place, rows), :]
-
-    rows_of = []
+        return elements[heights[source], pl.ds(4 * place, rows), :]
+
+    rows_of, heights, targets = [], places(HEIGHT_ORDER), places(JOIN_ORDER)
     for source in range(4):
         low, m, r = part(source, 2), part(source, 3), part(source, 6, 8)
         if source == 0:
@@ -162,7 +171,7 @@
                         kept[4 * comp + block, index - 1, place, :, lanes] = value
                 up, mp, low, m, rp, r = element
                 for place, value in enumerate((up, mp, low, m, *rp, *r)):
-                    sent[2 * (4 * comp + block) + half, place] = value
+                    sent[targets[2 * (4 * comp + block) + half], place] = value
 
 
 def tree(elements, first, last, keep):
@@ -187,8 +196,10 @@
 
 
 def chain_forward(received, sent, kept):
+    sources = places(JOIN_ORDER)
+
     def one(index):
-        up, mp, low, m, rp, r = (received[index, place] for place in range(6))
+        up, mp, low, m, rp, r = (received[sources[index], place] for place in range(6))
         return up, mp, low, m, [rp], [r]
 
     def keep(index, a, b, c):
@@ -202,10 +213,11 @@
 
 def chain_back(received, kept, sent, bound):
     groups, members = received.shape[0], sent.shape[0]
+    sources, targets = places(FAR_ORDER), places(BACK_ORDER)
     top = {}
 
     def one(index):
-        up, mp, low, m, rp, r = (received[index, place] for place in range(6))
+        up, mp, low, m, rp, r = (received[sources[index], place] for place in range(6))
         return up, mp, low, m, [rp], [r]
 
     def keep(index, a, b, c):
@@ -224,11 +236,11 @@
     before, value = bound[mine], bound[mine + 1]
 
     def end(index, value):
-        sent[index, 1] = value
+        sent[targets[index], 1] = value
         if index + 1 < members:
-            sent[index + 1, 0] = value
-
-    sent[0, 0] = before
+            sent[targets[index + 1], 0] = value
+
+    sent[targets[0], 0] = before
     end(members - 1, value)
     untree(lambda index: [kept[index, place] for place in range(3)], 0, members, before, value, end)
 
@@ -239,11 +251,13 @@
 
 
 def tunnel_back(received, kept, high, low, out, carried, solved, done):
+    sources = places(BACK_ORDER)
     for group in range(8):
         comp, block = group // 4, group % 4
         for half in range(2):
             lanes = pl.ds(half * LANES, LANES)
-            before, value = received[2 * group + half, 0], received[2 * group + half, 1]
+            source = sources[2 * group + half]
+            before, value = received[source, 0], received[source, 1]
             for index in range(3, -1, -1):
                 if index < 3:
                     a, b, c = (kept[group, index, place, :, lanes] for place in range(3))
@@ -325,11 +339,12 @@
 
 
 def per_device(cotangent, tun_cond, tun_flow, heat_loss, hgt_cond, hgt_lift, wid_cond):
-    members = 16
+    members = len(JOIN_ORDER)
     count = lax.axis_size("tun")
-    near = [list(range(first, first + members)) for first in range(0, count, members)]
-    far = [list(range(first, count, members)) for first in range(members)]
-    groups = len(near)
+    join = [[first + member for member in JOIN_ORDER] for first in range(0, count, members)]
+    back = [[first + member for member in BACK_ORDER] for first in range(0, count, members)]
+    far = [[first + members * group for group in FAR_ORDER] for first in range(members)]
+    groups = len(FAR_ORDER)
 
     def exchanged(value, axis, groups=None):
         return lax.all_to_all(value, axis, 0, 0, tiled=True, axis_index_groups=groups)
@@ -354,7 +369,7 @@
         wid_cond,
         place=pltpu.HBM,
     )
-    elements = exchanged(elements, "hgt")
+    elements = exchanged(elements, "hgt", [list(HEIGHT_ORDER)])
     sent, kept = call(
         height_back,
         [((members, 6, 8, LANES), F32), ((8, 3, 3, 8, 256), F32)],
@@ -366,7 +381,7 @@
         rows(tun_flow),
         rows(heat_loss),
     )
-    received = exchanged(sent, "tun", near)
+    received = exchanged(sent, "tun", join)
     sent, chain = call(
         chain_forward, [((groups, 6, 8, LANES), F32), ((members - 1, 3, 8, LANES), F32)], [], received
     )
@@ -374,7 +389,7 @@
     [sent] = call(
         chain_back, [((members, 2, 8, LANES), F32)], [room(groups + 1, 8, LANES)], received, chain
     )
-    received = exchanged(sent, "tun", near)
+    received = exchanged(sent, "tun", back)
     [solved] = call(
         tunnel_back,
         [((256, 256), F32)],

time: 72.4 us -> 63 us (0.87)
  blocking collectives: 68.2 us -> 58.8 us
    all_to_all x4, blocking collectives: 68.2 us -> 58.8 us  [exchanged(): lax.all_to_all(value, axis, 0, 0, tiled=True, axis_index_groups=groups)]
where the time goes in v4:
time: 63 us; the launch traced here: 62.7 us
  blocking collectives  58.8 us (93%)
  Pallas kernels  3.9 us (6%)
    all_to_all x4, blocking collectives, exchanged(): lax.all_to_all(value, axis, 0, 0, tiled=True, axis_index_groups=groups)  58.8 us
    pallas_call x5, Pallas kernels, call(): pl.pallas_call(kernel, out_shape=[jax.ShapeDtypeStruct(shape, dtype) for...  3.9 us

profile of v4, /device:TPU:1, one launch (start us, length us, event | category | flops | bytes accessed | tf_op | source)
XLA Modules:
  0.0 62.7 jit_solution(10777159917055562224)
XLA Ops:
  0.0 0.0 copy-start.2
  0.0 2.4 %shard_map.73 = (f32[4,32,256]{2,1,0:T(8,128)S(1)}, f32[4,15,8,256]{3,2,1,0:T(8,128)S(1)}, f32[16,256]{1,0:T(8,128)S(1)}, bf16[256,256]{1,0:T(8,128)(2,1)S(1)}, bf16[256,256]{1,0:T(8,128)(2,1)S(1)}) custom-call(f32[256,256]{1,0:T(8,128)} %bitcast.10, f32[128,256]{1,0:T(8,128)} %bitcast.11, f32[128,256]{1,0:T(8,128)} %bitcast.12, f32[257]{0:T(512)} %wide.1), custom_call_target="tpu_custom_call" | custom-call | tf_op jit(solution)/shard_map/pallas_call | solution.py:327
  2.4 0.0 copy-start
  2.4 0.0 copy-start.1
  2.5 8.4 %all_to_all.20.elements = f32[4,32,256]{2,1,0:T(8,128)S(1)} all-to-all(f32[4,32,256]{2,1,0:T(8,128)S(1)} %get-tuple-element.14), channel_id=1, replica_groups={{2,3,0,1},{6,7,4,5},{10,11,8,9},{14,15,12,13},{18,19,16,17},{22,23,20,2..., dimensions={0} | all-to-all | bytes 262144 | tf_op jit(solution)/shard_map/all_to_all | solution.py:350
  10.9 0.0 copy-done.2
  10.9 0.0 copy-done
  10.9 0.0 copy-done.1
  10.9 0.3 shard_map.74
  11.1 16.3 %all_to_all.21.received = f32[16,6,8,128]{3,2,1,0:T(8,128)S(1)} all-to-all(f32[16,6,8,128]{3,2,1,0:T(8,128)S(1)} %get-tuple-element.17), channel_id=1, replica_groups={{16,20,24,28,32,36,40,44,48,52,56,60,0,4,8,12},{80,84,88,92,96,100,104,..., dimensions={0} | all-to-all | bytes 786432 | tf_op jit(solution)/shard_map/all_to_all | solution.py:350
  27.5 0.1 shard_map.75
  27.6 20.5 %all_to_all.22.received = f32[8,6,8,128]{3,2,1,0:T(8,128)S(1)} all-to-all(f32[8,6,8,128]{3,2,1,0:T(8,128)S(1)} %get-tuple-element.18), channel_id=1, replica_groups={{320,384,448,0,64,128,192,256},{324,388,452,4,68,132,196,260},{328,392,..., dimensions={0} | all-to-all | bytes 393216 | tf_op jit(solution)/shard_map/all_to_all | solution.py:350
  48.0 0.1 shard_map.76
  48.1 13.6 %all_to_all.23.received = f32[16,2,8,128]{3,2,1,0:T(8,128)S(1)} all-to-all(f32[16,2,8,128]{3,2,1,0:T(8,128)S(1)} %shard_map.76), channel_id=1, replica_groups={{16,20,24,28,32,36,40,44,48,52,56,60,0,4,8,12},{80,84,88,92,96,100,104,..., dimensions={0} | all-to-all | bytes 262144 | tf_op jit(solution)/shard_map/all_to_all | solution.py:350
  61.7 1.1 %shard_map.77 = f32[256,256]{1,0:T(8,128)} custom-call(f32[16,2,8,128]{3,2,1,0:T(8,128)S(1)} %all_to_all.23.received, f32[8,3,3,8,256]{4,3,2,1,0:T(8,128)S(1)} %get-tuple-element.20.kept, bf16[256,256]{1,0:T(8,128)(2,1)S(1)} %get-tuple-element.21.high, bf16[256,256]{1,0:T(8,128)(2,1)S(1)} %get-tuple-element.22.low), custom_call_target="tpu_custom_call" | custom-call | tf_op jit(solution)/shard_map/pallas_call | solution.py:327
Async XLA Ops:
  0.0 10.9 %copy-start.2 = (f32[4,32,256]{2,1,0:T(8,128)S(1)}, f32[4,32,256]{2,1,0:T(8,128)}, u32[]{:S(2)}) copy-start(f32[4,32,256]{2,1,0:T(8,128)} %param.10) | copy-start | bytes 393220
  2.4 8.4 %copy-start = (f32[4,32,256]{2,1,0:T(8,128)S(1)}, f32[4,32,256]{2,1,0:T(8,128)}, u32[]{:S(2)}) copy-start(f32[4,32,256]{2,1,0:T(8,128)} %param.8) | copy-start | bytes 393220
  2.4 8.4 %copy-start.1 = (f32[4,32,256]{2,1,0:T(8,128)S(1)}, f32[4,32,256]{2,1,0:T(8,128)}, u32[]{:S(2)}) copy-start(f32[4,32,256]{2,1,0:T(8,128)} %param.9) | copy-start | bytes 393220

commit v5 on v4

--- a/solution.py
+++ b/solution.py
@@ -7,11 +7,12 @@
 
 F32 = jnp.float32
 LANES = 128
+EARLY_LAYERS = 6
 
 HEIGHT_ORDER = (2, 3, 0, 1)
-JOIN_ORDER = (4, 5, 6, 7, 8, 9, 10, 11, 12, 13, 14, 15, 0, 1, 2, 3)
+JOIN_ORDER = (13, 14, 15, 0, 1, 2, 3, 4, 5, 6, 7, 8, 9, 10, 11, 12)
 FAR_ORDER = (5, 6, 7, 0, 1, 2, 3, 4)
-BACK_ORDER = (4, 5, 6, 7, 8, 9, 10, 11, 12, 13, 14, 15, 0, 1, 2, 3)
+BACK_ORDER = (5, 6, 7, 8, 9, 10, 11, 12, 13, 14, 15, 0, 1, 2, 3, 4)
 
 
 def places(order):
@@ -36,7 +37,11 @@
     return whole, a, b, c
 
 
-def front(field, cond, lift, wide, elements, saved, middle, high, rest, pieces, fields, conds, lifts, face, done):
+def early():
+    return lax.axis_index("tun") // 8 < EARLY_LAYERS
+
+
+def front(field, cond, lift, wide, elements, saved, middle, high, rest, face, pieces, fields, conds, lifts, done):
     face_copy = pltpu.make_async_copy(wide, face, done.at[6])
     face_copy.start()
     copies = []
@@ -48,7 +53,11 @@
             copy.start()
             copies.append(copy)
     face_copy.wait()
-    width_inverse(face, high, rest)
+
+    @pl.when(early())
+    def _():
+        width_inverse(face, high, rest)
+
     for copy in copies:
         copy.wait()
     height_forward(elements, saved, middle, pieces, fields, conds, lifts)
@@ -250,7 +259,15 @@
     return high, (value - high.astype(F32)).astype(jnp.bfloat16)
 
 
-def tunnel_back(received, kept, high, low, out, carried, solved, done):
+def tunnel_back(received, kept, high, low, face, out, carried, solved, top_matrix, rest_matrix, done):
+    @pl.when(early())
+    def _():
+        top_matrix[...], rest_matrix[...] = high[...], low[...]
+
+    @pl.when(jnp.logical_not(early()))
+    def _():
+        width_inverse(face, top_matrix, rest_matrix)
+
     sources = places(BACK_ORDER)
     for group in range(8):
         comp, block = group // 4, group % 4
@@ -267,11 +284,12 @@
     def times(one, two):
         return jnp.dot(one, two[...], preferred_element_type=F32)
 
+    top, rest = split(carried[...])
+    both = times(jnp.concatenate([top, rest], axis=0), top_matrix)
+    solved[...] = both[:256] + (times(top, rest_matrix) + both[256:])
     copies = []
     for part in range(4):
         rows = pl.ds(64 * part, 64)
-        top, rest = split(carried[rows, :])
-        solved[rows, :] = times(top, high) + (times(top, low) + times(rest, high))
         copy = pltpu.make_async_copy(solved.at[rows, :], out.at[rows, :], done.at[part])
         copy.start()
         copies.append(copy)
@@ -352,15 +370,14 @@
     def rows(value):
         return value.reshape(-1, 256)
 
-    elements, saved, middle, high, low = call(
+    elements, saved, middle, high, low, face = call(
         front,
-        [((4, 32, 256), F32), ((4, 15, 8, 256), F32), ((16, 256), F32), *[((256, 256), jnp.bfloat16)] * 2],
+        [((4, 32, 256), F32), ((4, 15, 8, 256), F32), ((16, 256), F32), *[((256, 256), jnp.bfloat16)] * 2, ((257,), F32)],
         [
             room(2, 8, 8, LANES),
             room(2, 256, LANES),
             room(2, 128, LANES),
             room(2, 128, LANES),
-            room(257),
             pltpu.SemaphoreType.DMA((7,)),
         ],
         rows(cotangent),
@@ -393,11 +410,18 @@
     [solved] = call(
         tunnel_back,
         [((256, 256), F32)],
-        [room(256, 256), room(256, 256), pltpu.SemaphoreType.DMA((4,))],
+        [
+            room(256, 256),
+            room(256, 256),
+            pltpu.VMEM((256, 256), jnp.bfloat16),
+            pltpu.VMEM((256, 256), jnp.bfloat16),
+            pltpu.SemaphoreType.DMA((4,)),
+        ],
         received,
         kept,
         high,
         low,
+        face,
         out_place=pltpu.HBM,
     )
     return solved.reshape(cotangent.shape)

time: 63 us -> 60.7 us (0.963)
  blocking collectives: 58.8 us -> 56.5 us
    all_to_all x4, blocking collectives: 58.8 us -> 56.5 us  [exchanged(): lax.all_to_all(value, axis, 0, 0, tiled=True, axis_index_groups=groups)]
where the time goes in v5:
time: 60.7 us; the launch traced here: 60.5 us
  blocking collectives  56.5 us (93%)
  Pallas kernels  3.87 us (6%)
    all_to_all x4, blocking collectives, exchanged(): lax.all_to_all(value, axis, 0, 0, tiled=True, axis_index_groups=groups)  56.5 us
    pallas_call x5, Pallas kernels, call(): pl.pallas_call(kernel, out_shape=[jax.ShapeDtypeStruct(shape, dtype) for...  3.87 us

profile of v5, /device:TPU:1, one launch (start us, length us, event | category | flops | bytes accessed | tf_op | source)
XLA Modules:
  0.0 60.5 jit_solution(1999763036558024539)
XLA Ops:
  0.0 0.0 copy-start.2
  0.0 2.4 %shard_map.73 = (f32[4,32,256]{2,1,0:T(8,128)S(1)}, f32[4,15,8,256]{3,2,1,0:T(8,128)S(1)}, f32[16,256]{1,0:T(8,128)S(1)}, bf16[256,256]{1,0:T(8,128)(2,1)S(1)}, ...) custom-call(f32[256,256]{1,0:T(8,128)} %bitcast.10, f32[128,256]{1,0:T(8,128)} %bitcast.11, f32[128,256]{1,0:T(8,128)} %bitcast.12, ...), custom_call_target="tpu_custom_call" | custom-call | tf_op jit(solution)/shard_map/pallas_call | solution.py:345
  2.4 0.0 copy-start
  2.4 0.0 copy-start.1
  2.5 8.4 %all_to_all.20.elements = f32[4,32,256]{2,1,0:T(8,128)S(1)} all-to-all(f32[4,32,256]{2,1,0:T(8,128)S(1)} %get-tuple-element.15), channel_id=1, replica_groups={{2,3,0,1},{6,7,4,5},{10,11,8,9},{14,15,12,13},{18,19,16,17},{22,23,20,2..., dimensions={0} | all-to-all | bytes 262144 | tf_op jit(solution)/shard_map/all_to_all | solution.py:368
  10.9 0.0 copy-done.2
  10.9 0.0 copy-done
  10.9 0.0 copy-done.1
  10.9 0.3 shard_map.74
  11.1 16.1 %all_to_all.21.received = f32[16,6,8,128]{3,2,1,0:T(8,128)S(1)} all-to-all(f32[16,6,8,128]{3,2,1,0:T(8,128)S(1)} %get-tuple-element.18), channel_id=1, replica_groups={{52,56,60,0,4,8,12,16,20,24,28,32,36,40,44,48},{116,120,124,64,68,72,76..., dimensions={0} | all-to-all | bytes 786432 | tf_op jit(solution)/shard_map/all_to_all | solution.py:368
  27.2 0.1 shard_map.75
  27.3 18.1 %all_to_all.22.received = f32[8,6,8,128]{3,2,1,0:T(8,128)S(1)} all-to-all(f32[8,6,8,128]{3,2,1,0:T(8,128)S(1)} %get-tuple-element.19), channel_id=1, replica_groups={{320,384,448,0,64,128,192,256},{324,388,452,4,68,132,196,260},{328,392,..., dimensions={0} | all-to-all | bytes 393216 | tf_op jit(solution)/shard_map/all_to_all | solution.py:368
  45.4 0.1 shard_map.76
  45.4 14.0 %all_to_all.23.received = f32[16,2,8,128]{3,2,1,0:T(8,128)S(1)} all-to-all(f32[16,2,8,128]{3,2,1,0:T(8,128)S(1)} %shard_map.76), channel_id=1, replica_groups={{20,24,28,32,36,40,44,48,52,56,60,0,4,8,12,16},{84,88,92,96,100,104,108..., dimensions={0} | all-to-all | bytes 262144 | tf_op jit(solution)/shard_map/all_to_all | solution.py:368
  59.4 1.0 %shard_map.77 = f32[256,256]{1,0:T(8,128)} custom-call(f32[16,2,8,128]{3,2,1,0:T(8,128)S(1)} %all_to_all.23.received, f32[8,3,3,8,256]{4,3,2,1,0:T(8,128)S(1)} %get-tuple-element.21.kept, bf16[256,256]{1,0:T(8,128)(2,1)S(1)} %get-tuple-element.22.high, bf16[256,256]{1,0:T(8,128)(2,1)S(1)} %get-tuple-element.23.low, f32[257]{0:T(512)S(1)} %get-tuple-element.24.face), custom_call_target="tpu_custom_call" | custom-call | tf_op jit(solution)/shard_map/pallas_call | solution.py:345
Async XLA Ops:
  0.0 10.9 %copy-start.2 = (f32[4,32,256]{2,1,0:T(8,128)S(1)}, f32[4,32,256]{2,1,0:T(8,128)}, u32[]{:S(2)}) copy-start(f32[4,32,256]{2,1,0:T(8,128)} %param.10) | copy-start | bytes 393220
  2.4 8.4 %copy-start = (f32[4,32,256]{2,1,0:T(8,128)S(1)}, f32[4,32,256]{2,1,0:T(8,128)}, u32[]{:S(2)}) copy-start(f32[4,32,256]{2,1,0:T(8,128)} %param.8) | copy-start | bytes 393220
  2.4 8.4 %copy-start.1 = (f32[4,32,256]{2,1,0:T(8,128)S(1)}, f32[4,32,256]{2,1,0:T(8,128)}, u32[]{:S(2)}) copy-start(f32[4,32,256]{2,1,0:T(8,128)} %param.9) | copy-start | bytes 393220

commit v6 on v5

--- a/solution.py
+++ b/solution.py
@@ -10,9 +10,9 @@
 EARLY_LAYERS = 6
 
 HEIGHT_ORDER = (2, 3, 0, 1)
-JOIN_ORDER = (13, 14, 15, 0, 1, 2, 3, 4, 5, 6, 7, 8, 9, 10, 11, 12)
-FAR_ORDER = (5, 6, 7, 0, 1, 2, 3, 4)
-BACK_ORDER = (5, 6, 7, 8, 9, 10, 11, 12, 13, 14, 15, 0, 1, 2, 3, 4)
+JOIN_ORDER = (10, 11, 12, 13, 14, 15, 0, 1, 2, 3, 4, 5, 6, 7, 8, 9)
+FAR_ORDER = (2, 3, 0, 1)
+BACK_ORDER = (21, 22, 23, 24, 25, 26, 27, 28, 29, 30, 31, 0, 1, 2, 3, 4, 5, 6, 7, 8, 9, 10, 11, 12, 13, 14, 15, 16, 17, 18, 19, 20)
 
 
 def places(order):
@@ -109,7 +109,7 @@
     def part(source, place, rows=4):
         return elements[heights[source], pl.ds(4 * place, rows), :]
 
-    rows_of, heights, targets = [], places(HEIGHT_ORDER), places(JOIN_ORDER)
+    rows_of, heights = [], places(HEIGHT_ORDER)
     for source in range(4):
         low, m, r = part(source, 2), part(source, 3), part(source, 6, 8)
         if source == 0:
@@ -180,7 +180,7 @@
                         kept[4 * comp + block, index - 1, place, :, lanes] = value
                 up, mp, low, m, rp, r = element
                 for place, value in enumerate((up, mp, low, m, *rp, *r)):
-                    sent[targets[2 * (4 * comp + block) + half], place] = value
+                    sent[4 * comp + block, half, place] = value
 
 
 def tree(elements, first, last, keep):
@@ -204,54 +204,76 @@
     untree(kept, centre, last, middle, value, give)
 
 
+def element_at(ref, *index):
+    up, mp, low, m, rp, r = (ref[(*index, pl.ds(4 * place, 4))] for place in range(6))
+    return up, mp, low, m, [rp], [r]
+
+
+def listed(element):
+    up, mp, low, m, rp, r = element
+    return up, mp, low, m, *rp, *r
+
+
+def pair_forward(received, sent, kept):
+    targets = places(JOIN_ORDER)
+    core = lax.axis_index("tun") % 2
+
+    def one(which, group, half):
+        up, mp, low, m, rp, r = (received[which, group, half, place] for place in range(6))
+        return up, mp, low, m, [rp], [r]
+
+    for group in range(8):
+        for half in range(2):
+            _, a, b, c = joined(one(0, group, half), one(1, group, half))
+            kept[group, half, 0], kept[group, half, 1], kept[group, half, 2] = a, b, c[0]
+        whole = joined(one(0, group, core), one(1, group, core))[0]
+        for place, value in enumerate(listed(whole)):
+            for part in range(2):
+                sent[targets[2 * group + part], pl.ds(4 * place, 4)] = value[4 * part : 4 * part + 4]
+
+
 def chain_forward(received, sent, kept):
     sources = places(JOIN_ORDER)
 
-    def one(index):
-        up, mp, low, m, rp, r = (received[sources[index], place] for place in range(6))
-        return up, mp, low, m, [rp], [r]
-
     def keep(index, a, b, c):
         kept[index, 0], kept[index, 1], kept[index, 2] = a, b, c[0]
 
-    up, mp, low, m, rp, r = tree(one, 0, received.shape[0], keep)
-    for place, value in enumerate((up, mp, low, m, *rp, *r)):
+    whole = tree(lambda index: element_at(received, sources[index]), 0, received.shape[0], keep)
+    for place, value in enumerate(listed(whole)):
         for target in range(sent.shape[0]):
-            sent[target, place] = value
+            sent[target, pl.ds(4 * place, 4)] = value
 
 
 def chain_back(received, kept, sent, bound):
-    groups, members = received.shape[0], sent.shape[0]
+    groups, chips = received.shape[0], sent.shape[0] // 2
     sources, targets = places(FAR_ORDER), places(BACK_ORDER)
     top = {}
 
-    def one(index):
-        up, mp, low, m, rp, r = (received[sources[index], place] for place in range(6))
-        return up, mp, low, m, [rp], [r]
-
     def keep(index, a, b, c):
         top[index] = a, b, c[0]
 
     def give(index, value):
         bound[index + 1] = value
 
-    up, mp, low, m, rp, r = tree(one, 0, groups, keep)
+    up, mp, low, m, rp, r = tree(lambda index: element_at(received, sources[index]), 0, groups, keep)
     zero = jnp.zeros_like(up)
     value = r[0] / (low + m)
     bound[0] = zero
     give(groups - 1, value)
     untree(lambda index: top[index], 0, groups, zero, value, give)
-    mine = lax.axis_index("tun") // members
+    mine = lax.axis_index("tun") // (2 * chips)
     before, value = bound[mine], bound[mine + 1]
 
     def end(index, value):
-        sent[targets[index], 1] = value
-        if index + 1 < members:
-            sent[targets[index + 1], 0] = value
-
-    sent[targets[0], 0] = before
-    end(members - 1, value)
-    untree(lambda index: [kept[index, place] for place in range(3)], 0, members, before, value, end)
+        for core in range(2):
+            sent[targets[2 * index + core], 4:8] = value
+            if index + 1 < chips:
+                sent[targets[2 * index + 2 + core], 0:4] = value
+
+    for core in range(2):
+        sent[targets[core], 0:4] = before
+    end(chips - 1, value)
+    untree(lambda index: [kept[index, place] for place in range(3)], 0, chips, before, value, end)
 
 
 def split(value):
@@ -259,7 +281,7 @@
     return high, (value - high.astype(F32)).astype(jnp.bfloat16)
 
 
-def tunnel_back(received, kept, high, low, face, out, carried, solved, top_matrix, rest_matrix, done):
+def tunnel_back(received, paired, kept, high, low, face, out, carried, solved, top_matrix, rest_matrix, done):
     @pl.when(early())
     def _():
         top_matrix[...], rest_matrix[...] = high[...], low[...]
@@ -269,12 +291,18 @@
         width_inverse(face, top_matrix, rest_matrix)
 
     sources = places(BACK_ORDER)
+    first = lax.axis_index("tun") % 2 == 0
     for group in range(8):
         comp, block = group // 4, group % 4
         for half in range(2):
             lanes = pl.ds(half * LANES, LANES)
-            source = sources[2 * group + half]
-            before, value = received[source, 0], received[source, 1]
+            parts = [sources[4 * group + 2 * part + half] for part in range(2)]
+            before, value = (
+                jnp.concatenate([received[part, pl.ds(start, 4)] for part in parts], axis=0) for start in (0, 4)
+            )
+            a, b, c = (paired[group, half, place] for place in range(3))
+            centre = c + a * before + b * value
+            before, value = jnp.where(first, before, centre), jnp.where(first, centre, value)
             for index in range(3, -1, -1):
                 if index < 3:
                     a, b, c = (kept[group, index, place, :, lanes] for place in range(3))
@@ -357,9 +385,10 @@
 
 
 def per_device(cotangent, tun_cond, tun_flow, heat_loss, hgt_cond, hgt_lift, wid_cond):
-    members = len(JOIN_ORDER)
+    chips, members = len(JOIN_ORDER), len(BACK_ORDER)
     count = lax.axis_size("tun")
-    join = [[first + member for member in JOIN_ORDER] for first in range(0, count, members)]
+    cores = [[first, first + 1] for first in range(0, count, 2)]
+    join = [[first + 2 * chip + core for chip in JOIN_ORDER] for first in range(0, count, members) for core in range(2)]
     back = [[first + member for member in BACK_ORDER] for first in range(0, count, members)]
     far = [[first + members * group for group in FAR_ORDER] for first in range(members)]
     groups = len(FAR_ORDER)
@@ -389,7 +418,7 @@
     elements = exchanged(elements, "hgt", [list(HEIGHT_ORDER)])
     sent, kept = call(
         height_back,
-        [((members, 6, 8, LANES), F32), ((8, 3, 3, 8, 256), F32)],
+        [((8, 2, 6, 8, LANES), F32), ((8, 3, 3, 8, 256), F32)],
         [room(5, 8, 256), room(2, 2, 2, 8, LANES), room(2, 256, LANES)],
         elements,
         saved,
@@ -398,14 +427,16 @@
         rows(tun_flow),
         rows(heat_loss),
     )
+    received = lax.all_gather(sent, "tun", axis_index_groups=cores)
+    sent, paired = call(
+        pair_forward, [((chips, 24, LANES), F32), ((8, 2, 3, 8, LANES), F32)], [], received
+    )
     received = exchanged(sent, "tun", join)
     sent, chain = call(
-        chain_forward, [((groups, 6, 8, LANES), F32), ((members - 1, 3, 8, LANES), F32)], [], received
+        chain_forward, [((groups, 24, LANES), F32), ((chips - 1, 3, 4, LANES), F32)], [], received
     )
     received = exchanged(sent, "tun", far)
-    [sent] = call(
-        chain_back, [((members, 2, 8, LANES), F32)], [room(groups + 1, 8, LANES)], received, chain
-    )
+    [sent] = call(chain_back, [((members, 8, LANES), F32)], [room(groups + 1, 4, LANES)], received, chain)
     received = exchanged(sent, "tun", back)
     [solved] = call(
         tunnel_back,
@@ -418,6 +449,7 @@
             pltpu.SemaphoreType.DMA((4,)),
         ],
         received,
+        paired,
         kept,
         high,
         low,

time: 60.7 us -> 59 us (0.972)
  blocking collectives: 56.5 us -> 54.7 us
    all_to_all x4, blocking collectives: 56.5 us -> 46.7 us  [exchanged(): lax.all_to_all(value, axis, 0, 0, tiled=True, axis_index_groups=groups)]
    all_gather x0 -> x1, blocking collectives: none -> 8.01 us  [per_device(): received = lax.all_gather(sent, 'tun', axis_index_groups=cores)]
    pallas_call x5 -> x6, Pallas kernels: 3.87 us -> 3.93 us  [call(): pl.pallas_call(kernel, out_shape=[jax.ShapeDtypeStruct(shape, dtype) for...]
where the time goes in v6:
time: 59 us; the launch traced here: 58.7 us
  blocking collectives  54.7 us (93%)
  Pallas kernels  3.93 us (7%)
    all_to_all x4, blocking collectives, exchanged(): lax.all_to_all(value, axis, 0, 0, tiled=True, axis_index_groups=groups)  46.7 us
    all_gather x1, blocking collectives, per_device(): received = lax.all_gather(sent, 'tun', axis_index_groups=cores)  8.01 us
    pallas_call x6, Pallas kernels, call(): pl.pallas_call(kernel, out_shape=[jax.ShapeDtypeStruct(shape, dtype) for...  3.93 us

profile of v6, /device:TPU:1, one launch (start us, length us, event | category | flops | bytes accessed | tf_op | source)
XLA Modules:
  0.0 58.7 jit_solution(729397455451176299)
XLA Ops:
  0.0 0.0 copy-start.2
  0.0 2.4 %shard_map.73 = (f32[4,32,256]{2,1,0:T(8,128)S(1)}, f32[4,15,8,256]{3,2,1,0:T(8,128)S(1)}, f32[16,256]{1,0:T(8,128)S(1)}, bf16[256,256]{1,0:T(8,128)(2,1)S(1)}, ...) custom-call(f32[256,256]{1,0:T(8,128)} %bitcast.12, f32[128,256]{1,0:T(8,128)} %bitcast.13, f32[128,256]{1,0:T(8,128)} %bitcast.14, ...), custom_call_target="tpu_custom_call" | custom-call | tf_op jit(solution)/shard_map/pallas_call | solution.py:373
  2.4 0.0 copy-start
  2.4 0.0 copy-start.1
  2.5 8.4 %all_to_all.20.elements = f32[4,32,256]{2,1,0:T(8,128)S(1)} all-to-all(f32[4,32,256]{2,1,0:T(8,128)S(1)} %get-tuple-element.17), channel_id=1, replica_groups={{2,3,0,1},{6,7,4,5},{10,11,8,9},{14,15,12,13},{18,19,16,17},{22,23,20,2..., dimensions={0} | all-to-all | bytes 262144 | tf_op jit(solution)/shard_map/all_to_all | solution.py:397
  10.9 0.0 copy-done.2
  10.9 0.0 copy-done
  10.9 0.0 copy-done.1
  10.9 0.3 shard_map.74
  11.1 8.0 %all-gather = f32[16,2,6,8,128]{4,3,2,1,0:T(8,128)S(1)} all-gather(f32[8,2,6,8,128]{4,3,2,1,0:T(8,128)S(1)} %get-tuple-element.20), channel_id=2, replica_groups={{0,4},{8,12},{16,20},{24,28},{32,36},{40,44},{48,52},{56,60},{64,68},{7..., dimensions={0}, use_global_device_ids=true | all-gather | bytes 1179648 | tf_op jit(solution)/shard_map/all_gather | solution.py:430
  19.1 0.1 shard_map.75
  19.2 10.2 %all_to_all.21.received = f32[16,24,128]{2,1,0:T(8,128)S(1)} all-to-all(f32[16,24,128]{2,1,0:T(8,128)S(1)} %get-tuple-element.21), channel_id=1, replica_groups={{80,88,96,104,112,120,0,8,16,24,32,40,48,56,64,72},{84,92,100,108,116,1..., dimensions={0} | all-to-all | bytes 393216 | tf_op jit(solution)/shard_map/all_to_all | solution.py:397
  29.4 0.1 shard_map.76
  29.5 14.3 %all_to_all.22.received = f32[4,24,128]{2,1,0:T(8,128)S(1)} all-to-all(f32[4,24,128]{2,1,0:T(8,128)S(1)} %get-tuple-element.22), channel_id=1, replica_groups={{256,384,0,128},{260,388,4,132},{264,392,8,136},{268,396,12,140},{272,4..., dimensions={0} | all-to-all | bytes 98304 | tf_op jit(solution)/shard_map/all_to_all | solution.py:397
  43.8 0.1 shard_map.77
  43.9 13.8 %all_to_all.23.received = f32[32,8,128]{2,1,0:T(8,128)S(1)} all-to-all(f32[32,8,128]{2,1,0:T(8,128)S(1)} %shard_map.77), channel_id=1, replica_groups={{84,88,92,96,100,104,108,112,116,120,124,0,4,8,12,16,20,24,28,32,36,40,..., dimensions={0} | all-to-all | bytes 262144 | tf_op jit(solution)/shard_map/all_to_all | solution.py:397
  57.7 1.1 %shard_map.78 = f32[256,256]{1,0:T(8,128)} custom-call(f32[32,8,128]{2,1,0:T(8,128)S(1)} %all_to_all.23.received, f32[8,2,3,8,128]{4,3,2,1,0:T(8,128)S(1)} %get-tuple-element.24.paired, f32[8,3,3,8,256]{4,3,2,1,0:T(8,128)S(1)} %get-tuple-element.25.kept, bf16[256,256]{1,0:T(8,128)(2,1)S(1)} %get-tuple-element.26.high, ...), custom_call_target="tpu_custom_call" | custom-call | tf_op jit(solution)/shard_map/pallas_call | solution.py:373
Async XLA Ops:
  0.0 10.9 %copy-start.2 = (f32[4,32,256]{2,1,0:T(8,128)S(1)}, f32[4,32,256]{2,1,0:T(8,128)}, u32[]{:S(2)}) copy-start(f32[4,32,256]{2,1,0:T(8,128)} %param.10) | copy-start | bytes 393220
  2.4 8.4 %copy-start = (f32[4,32,256]{2,1,0:T(8,128)S(1)}, f32[4,32,256]{2,1,0:T(8,128)}, u32[]{:S(2)}) copy-start(f32[4,32,256]{2,1,0:T(8,128)} %param.8) | copy-start | bytes 393220
  2.4 8.4 %copy-start.1 = (f32[4,32,256]{2,1,0:T(8,128)S(1)}, f32[4,32,256]{2,1,0:T(8,128)}, u32[]{:S(2)}) copy-start(f32[4,32,256]{2,1,0:T(8,128)} %param.9) | copy-start | bytes 393220

commit v7 on v6

--- a/solution.py
+++ b/solution.py
@@ -10,7 +10,7 @@
 EARLY_LAYERS = 6
 
 HEIGHT_ORDER = (2, 3, 0, 1)
-JOIN_ORDER = (10, 11, 12, 13, 14, 15, 0, 1, 2, 3, 4, 5, 6, 7, 8, 9)
+JOIN_ORDER = (10, 6, 9, 11, 14, 5, 7, 13, 15, 1, 2, 3, 0, 4, 8, 12)
 FAR_ORDER = (2, 3, 0, 1)
 BACK_ORDER = (21, 22, 23, 24, 25, 26, 27, 28, 29, 30, 31, 0, 1, 2, 3, 4, 5, 6, 7, 8, 9, 10, 11, 12, 13, 14, 15, 16, 17, 18, 19, 20)
 

time: 59 us -> 58.6 us (level)
  no operation moved by 1% of the time
where the time goes in v7:
time: 58.6 us; the launch traced here: 58.3 us
  blocking collectives  54.3 us (93%)
  Pallas kernels  3.93 us (7%)
    all_to_all x4, blocking collectives, exchanged(): lax.all_to_all(value, axis, 0, 0, tiled=True, axis_index_groups=groups)  46.3 us
    all_gather x1, blocking collectives, per_device(): received = lax.all_gather(sent, 'tun', axis_index_groups=cores)  8.01 us
    pallas_call x6, Pallas kernels, call(): pl.pallas_call(kernel, out_shape=[jax.ShapeDtypeStruct(shape, dtype) for...  3.93 us

profile of v7, /device:TPU:1, one launch (start us, length us, event | category | flops | bytes accessed | tf_op | source)
XLA Modules:
  0.0 58.3 jit_solution(3550016121690354742)
XLA Ops:
  0.0 0.0 copy-start.2
  0.0 2.4 %shard_map.73 = (f32[4,32,256]{2,1,0:T(8,128)S(1)}, f32[4,15,8,256]{3,2,1,0:T(8,128)S(1)}, f32[16,256]{1,0:T(8,128)S(1)}, bf16[256,256]{1,0:T(8,128)(2,1)S(1)}, ...) custom-call(f32[256,256]{1,0:T(8,128)} %bitcast.12, f32[128,256]{1,0:T(8,128)} %bitcast.13, f32[128,256]{1,0:T(8,128)} %bitcast.14, ...), custom_call_target="tpu_custom_call" | custom-call | tf_op jit(solution)/shard_map/pallas_call | solution.py:373
  2.4 0.0 copy-start
  2.4 0.0 copy-start.1
  2.5 8.4 %all_to_all.20.elements = f32[4,32,256]{2,1,0:T(8,128)S(1)} all-to-all(f32[4,32,256]{2,1,0:T(8,128)S(1)} %get-tuple-element.17), channel_id=1, replica_groups={{2,3,0,1},{6,7,4,5},{10,11,8,9},{14,15,12,13},{18,19,16,17},{22,23,20,2..., dimensions={0} | all-to-all | bytes 262144 | tf_op jit(solution)/shard_map/all_to_all | solution.py:397
  10.9 0.0 copy-done.2
  10.9 0.0 copy-done
  10.9 0.0 copy-done.1
  10.9 0.3 shard_map.74
  11.1 8.0 %all-gather = f32[16,2,6,8,128]{4,3,2,1,0:T(8,128)S(1)} all-gather(f32[8,2,6,8,128]{4,3,2,1,0:T(8,128)S(1)} %get-tuple-element.20), channel_id=2, replica_groups={{0,4},{8,12},{16,20},{24,28},{32,36},{40,44},{48,52},{56,60},{64,68},{7..., dimensions={0}, use_global_device_ids=true | all-gather | bytes 1179648 | tf_op jit(solution)/shard_map/all_gather | solution.py:430
  19.1 0.1 shard_map.75
  19.2 10.0 %all_to_all.21.received = f32[16,24,128]{2,1,0:T(8,128)S(1)} all-to-all(f32[16,24,128]{2,1,0:T(8,128)S(1)} %get-tuple-element.21), channel_id=1, replica_groups={{80,48,72,88,112,40,56,104,120,8,16,24,0,32,64,96},{84,52,76,92,116,44,..., dimensions={0} | all-to-all | bytes 393216 | tf_op jit(solution)/shard_map/all_to_all | solution.py:397
  29.2 0.1 shard_map.76
  29.3 13.9 %all_to_all.22.received = f32[4,24,128]{2,1,0:T(8,128)S(1)} all-to-all(f32[4,24,128]{2,1,0:T(8,128)S(1)} %get-tuple-element.22), channel_id=1, replica_groups={{256,384,0,128},{260,388,4,132},{264,392,8,136},{268,396,12,140},{272,4..., dimensions={0} | all-to-all | bytes 98304 | tf_op jit(solution)/shard_map/all_to_all | solution.py:397
  43.2 0.1 shard_map.77
  43.2 14.0 %all_to_all.23.received = f32[32,8,128]{2,1,0:T(8,128)S(1)} all-to-all(f32[32,8,128]{2,1,0:T(8,128)S(1)} %shard_map.77), channel_id=1, replica_groups={{84,88,92,96,100,104,108,112,116,120,124,0,4,8,12,16,20,24,28,32,36,40,..., dimensions={0} | all-to-all | bytes 262144 | tf_op jit(solution)/shard_map/all_to_all | solution.py:397
  57.3 1.1 %shard_map.78 = f32[256,256]{1,0:T(8,128)} custom-call(f32[32,8,128]{2,1,0:T(8,128)S(1)} %all_to_all.23.received, f32[8,2,3,8,128]{4,3,2,1,0:T(8,128)S(1)} %get-tuple-element.24.paired, f32[8,3,3,8,256]{4,3,2,1,0:T(8,128)S(1)} %get-tuple-element.25.kept, bf16[256,256]{1,0:T(8,128)(2,1)S(1)} %get-tuple-element.26.high, ...), custom_call_target="tpu_custom_call" | custom-call | tf_op jit(solution)/shard_map/pallas_call | solution.py:373
Async XLA Ops:
  0.0 10.9 %copy-start.2 = (f32[4,32,256]{2,1,0:T(8,128)S(1)}, f32[4,32,256]{2,1,0:T(8,128)}, u32[]{:S(2)}) copy-start(f32[4,32,256]{2,1,0:T(8,128)} %param.10) | copy-start | bytes 393220
  2.4 8.4 %copy-start = (f32[4,32,256]{2,1,0:T(8,128)S(1)}, f32[4,32,256]{2,1,0:T(8,128)}, u32[]{:S(2)}) copy-start(f32[4,32,256]{2,1,0:T(8,128)} %param.8) | copy-start | bytes 393220
  2.4 8.4 %copy-start.1 = (f32[4,32,256]{2,1,0:T(8,128)S(1)}, f32[4,32,256]{2,1,0:T(8,128)}, u32[]{:S(2)}) copy-start(f32[4,32,256]{2,1,0:T(8,128)} %param.9) | copy-start | bytes 393220

commit v8 on v7

--- a/solution.py
+++ b/solution.py
@@ -227,9 +227,15 @@
             _, a, b, c = joined(one(0, group, half), one(1, group, half))
             kept[group, half, 0], kept[group, half, 1], kept[group, half, 2] = a, b, c[0]
         whole = joined(one(0, group, core), one(1, group, core))[0]
-        for place, value in enumerate(listed(whole)):
-            for part in range(2):
-                sent[targets[2 * group + part], pl.ds(4 * place, 4)] = value[4 * part : 4 * part + 4]
+        comp, block = group // 4, group % 4
+        up, mp, low, m, rp, r = listed(whole)
+        values = [up, mp, m, rp, r]
+        for part in range(4):
+            rows = slice(2 * part, 2 * part + 2)
+            for place, value in enumerate(values):
+                sent[targets[4 * block + part], 2 * place + comp] = value[rows]
+            if comp == 0:
+                sent[targets[4 * block + part], 10] = low[rows]
 
 
 def chain_forward(received, sent, kept):
@@ -238,7 +244,15 @@
     def keep(index, a, b, c):
         kept[index, 0], kept[index, 1], kept[index, 2] = a, b, c[0]
 
-    whole = tree(lambda index: element_at(received, sources[index]), 0, received.shape[0], keep)
+    def one(index):
+        source = sources[index]
+        pairs = [(received[source, 2 * place], received[source, 2 * place + 1]) for place in range(5)]
+        first = received[source, 10]
+        low = jnp.concatenate([first, first * (pairs[0][1] / pairs[0][0])], axis=0)
+        up, mp, m, rp, r = (jnp.concatenate(pair, axis=0) for pair in pairs)
+        return up, mp, low, m, [rp], [r]
+
+    whole = tree(one, 0, received.shape[0], keep)
     for place, value in enumerate(listed(whole)):
         for target in range(sent.shape[0]):
             sent[target, pl.ds(4 * place, 4)] = value
@@ -296,9 +310,10 @@
         comp, block = group // 4, group % 4
         for half in range(2):
             lanes = pl.ds(half * LANES, LANES)
-            parts = [sources[4 * group + 2 * part + half] for part in range(2)]
+            parts = [sources[8 * block + 2 * part + half] for part in range(4)]
             before, value = (
-                jnp.concatenate([received[part, pl.ds(start, 4)] for part in parts], axis=0) for start in (0, 4)
+                jnp.concatenate([received[part, pl.ds(start + 2 * comp, 2)] for part in parts], axis=0)
+                for start in (0, 4)
             )
             a, b, c = (paired[group, half, place] for place in range(3))
             centre = c + a * before + b * value
@@ -429,7 +444,7 @@
     )
     received = lax.all_gather(sent, "tun", axis_index_groups=cores)
     sent, paired = call(
-        pair_forward, [((chips, 24, LANES), F32), ((8, 2, 3, 8, LANES), F32)], [], received
+        pair_forward, [((chips, 11, 2, LANES), F32), ((8, 2, 3, 8, LANES), F32)], [], received
     )
     received = exchanged(sent, "tun", join)
     sent, chain = call(

time: 58.6 us -> 58.4 us (level)
  no operation moved by 1% of the time
where the time goes in v8:
time: 58.4 us; the launch traced here: 58.1 us
  blocking collectives  54 us (92%)
  Pallas kernels  4 us (7%)
    all_to_all x4, blocking collectives, exchanged(): lax.all_to_all(value, axis, 0, 0, tiled=True, axis_index_groups=groups)  46 us
    all_gather x1, blocking collectives, per_device(): received = lax.all_gather(sent, 'tun', axis_index_groups=cores)  8.01 us
    pallas_call x6, Pallas kernels, call(): pl.pallas_call(kernel, out_shape=[jax.ShapeDtypeStruct(shape, dtype) for...  4 us

profile of v8, /device:TPU:1, one launch (start us, length us, event | category | flops | bytes accessed | tf_op | source)
XLA Modules:
  0.0 58.1 jit_solution(15882174525838215037)
XLA Ops:
  0.0 0.0 copy-start.2
  0.0 2.4 %shard_map.73 = (f32[4,32,256]{2,1,0:T(8,128)S(1)}, f32[4,15,8,256]{3,2,1,0:T(8,128)S(1)}, f32[16,256]{1,0:T(8,128)S(1)}, bf16[256,256]{1,0:T(8,128)(2,1)S(1)}, ...) custom-call(f32[256,256]{1,0:T(8,128)} %bitcast.12, f32[128,256]{1,0:T(8,128)} %bitcast.13, f32[128,256]{1,0:T(8,128)} %bitcast.14, ...), custom_call_target="tpu_custom_call" | custom-call | tf_op jit(solution)/shard_map/pallas_call | solution.py:388
  2.4 0.0 copy-start
  2.4 0.0 copy-start.1
  2.5 8.4 %all_to_all.20.elements = f32[4,32,256]{2,1,0:T(8,128)S(1)} all-to-all(f32[4,32,256]{2,1,0:T(8,128)S(1)} %get-tuple-element.17), channel_id=1, replica_groups={{2,3,0,1},{6,7,4,5},{10,11,8,9},{14,15,12,13},{18,19,16,17},{22,23,20,2..., dimensions={0} | all-to-all | bytes 262144 | tf_op jit(solution)/shard_map/all_to_all | solution.py:412
  10.9 0.0 copy-done.2
  10.9 0.0 copy-done
  10.9 0.0 copy-done.1
  10.9 0.3 shard_map.74
  11.1 8.0 %all-gather = f32[16,2,6,8,128]{4,3,2,1,0:T(8,128)S(1)} all-gather(f32[8,2,6,8,128]{4,3,2,1,0:T(8,128)S(1)} %get-tuple-element.20), channel_id=2, replica_groups={{0,4},{8,12},{16,20},{24,28},{32,36},{40,44},{48,52},{56,60},{64,68},{7..., dimensions={0}, use_global_device_ids=true | all-gather | bytes 1179648 | tf_op jit(solution)/shard_map/all_gather | solution.py:445
  19.1 0.1 shard_map.75
  19.2 9.8 %all_to_all.21.received = f32[16,11,2,128]{3,2,1,0:T(2,128)S(1)} all-to-all(f32[16,11,2,128]{3,2,1,0:T(2,128)S(1)} %get-tuple-element.21), channel_id=1, replica_groups={{80,48,72,88,112,40,56,104,120,8,16,24,0,32,64,96},{84,52,76,92,116,44,..., dimensions={0} | all-to-all | bytes 360448 | tf_op jit(solution)/shard_map/all_to_all | solution.py:412
  29.0 0.1 shard_map.76
  29.1 13.9 %all_to_all.22.received = f32[4,24,128]{2,1,0:T(8,128)S(1)} all-to-all(f32[4,24,128]{2,1,0:T(8,128)S(1)} %get-tuple-element.22), channel_id=1, replica_groups={{256,384,0,128},{260,388,4,132},{264,392,8,136},{268,396,12,140},{272,4..., dimensions={0} | all-to-all | bytes 98304 | tf_op jit(solution)/shard_map/all_to_all | solution.py:412
  43.0 0.1 shard_map.77
  43.1 14.0 %all_to_all.23.received = f32[32,8,128]{2,1,0:T(8,128)S(1)} all-to-all(f32[32,8,128]{2,1,0:T(8,128)S(1)} %shard_map.77), channel_id=1, replica_groups={{84,88,92,96,100,104,108,112,116,120,124,0,4,8,12,16,20,24,28,32,36,40,..., dimensions={0} | all-to-all | bytes 262144 | tf_op jit(solution)/shard_map/all_to_all | solution.py:412
  57.0 1.1 %shard_map.78 = f32[256,256]{1,0:T(8,128)} custom-call(f32[32,8,128]{2,1,0:T(8,128)S(1)} %all_to_all.23.received, f32[8,2,3,8,128]{4,3,2,1,0:T(8,128)S(1)} %get-tuple-element.24.paired, f32[8,3,3,8,256]{4,3,2,1,0:T(8,128)S(1)} %get-tuple-element.25.kept, bf16[256,256]{1,0:T(8,128)(2,1)S(1)} %get-tuple-element.26.high, ...), custom_call_target="tpu_custom_call" | custom-call | tf_op jit(solution)/shard_map/pallas_call | solution.py:388
Async XLA Ops:
  0.0 10.9 %copy-start.2 = (f32[4,32,256]{2,1,0:T(8,128)S(1)}, f32[4,32,256]{2,1,0:T(8,128)}, u32[]{:S(2)}) copy-start(f32[4,32,256]{2,1,0:T(8,128)} %param.10) | copy-start | bytes 393220
  2.4 8.4 %copy-start = (f32[4,32,256]{2,1,0:T(8,128)S(1)}, f32[4,32,256]{2,1,0:T(8,128)}, u32[]{:S(2)}) copy-start(f32[4,32,256]{2,1,0:T(8,128)} %param.8) | copy-start | bytes 393220
  2.4 8.4 %copy-start.1 = (f32[4,32,256]{2,1,0:T(8,128)S(1)}, f32[4,32,256]{2,1,0:T(8,128)}, u32[]{:S(2)}) copy-start(f32[4,32,256]{2,1,0:T(8,128)} %param.9) | copy-start | bytes 393220

commit v9 on v8

--- a/solution.py
+++ b/solution.py
@@ -83,12 +83,11 @@
                 [cell(fields, index), cell(fields, index, 128)],
             )
 
-        element = one(0)
-        for index in range(1, 16):
-            element, a, b, c = joined(element, one(index))
+        def keep(index, a, b, c):
             for place, part in enumerate((a, b, *c)):
-                saved[place, index - 1, :, lanes] = part
-        up, mp, low, m, rp, r = element
+                saved[place, index, :, lanes] = part
+
+        up, mp, low, m, rp, r = tree(one, 0, 16, keep)
         for place, part in enumerate((up, mp, low, m, *rp, *r)):
             pieces[half, place] = part
 
@@ -153,13 +152,14 @@
             ends[half, comp, 1, odd] = last[rows, cut]
             start, value = ends[half, comp, 0], ends[half, comp, 1]
             lifted[half, pl.ds(128 * comp + 15, 8, stride=16), :] = value
-            for index in range(14, -1, -1):
-                value = (
-                    saved[2 + comp, index, :, lanes]
-                    + saved[0, index, :, lanes] * start
-                    + saved[1, index, :, lanes] * value
-                )
-                lifted[half, pl.ds(128 * comp + index, 8, stride=16), :] = value
+
+            def give(index, cell):
+                lifted[half, pl.ds(128 * comp + index, 8, stride=16), :] = cell
+
+            def parts(index):
+                return [saved[place, index, :, lanes] for place in (0, 1, 2 + comp)]
+
+            untree(parts, 0, 16, start, value, give)
     for block in range(4):
         for half in range(2):
             lanes = pl.ds(half * LANES, LANES)

time: 58.4 us -> 58.3 us (level)
  no operation moved by 1% of the time
where the time goes in v9:
time: 58.3 us; the launch traced here: 58.1 us
  blocking collectives  54 us (93%)
  Pallas kernels  3.96 us (7%)
    all_to_all x4, blocking collectives, exchanged(): lax.all_to_all(value, axis, 0, 0, tiled=True, axis_index_groups=groups)  46 us
    all_gather x1, blocking collectives, per_device(): received = lax.all_gather(sent, 'tun', axis_index_groups=cores)  8.01 us
    pallas_call x6, Pallas kernels, call(): pl.pallas_call(kernel, out_shape=[jax.ShapeDtypeStruct(shape, dtype) for...  3.96 us

profile of v9, /device:TPU:1, one launch (start us, length us, event | category | flops | bytes accessed | tf_op | source)
XLA Modules:
  0.0 58.1 jit_solution(4750155195438323270)
XLA Ops:
  0.0 0.0 copy-start.2
  0.0 2.4 %shard_map.73 = (f32[4,32,256]{2,1,0:T(8,128)S(1)}, f32[4,15,8,256]{3,2,1,0:T(8,128)S(1)}, f32[16,256]{1,0:T(8,128)S(1)}, bf16[256,256]{1,0:T(8,128)(2,1)S(1)}, ...) custom-call(f32[256,256]{1,0:T(8,128)} %bitcast.12, f32[128,256]{1,0:T(8,128)} %bitcast.13, f32[128,256]{1,0:T(8,128)} %bitcast.14, ...), custom_call_target="tpu_custom_call" | custom-call | tf_op jit(solution)/shard_map/pallas_call | solution.py:388
  2.4 0.0 copy-start
  2.4 0.0 copy-start.1
  2.4 8.4 %all_to_all.20.elements = f32[4,32,256]{2,1,0:T(8,128)S(1)} all-to-all(f32[4,32,256]{2,1,0:T(8,128)S(1)} %get-tuple-element.17), channel_id=1, replica_groups={{2,3,0,1},{6,7,4,5},{10,11,8,9},{14,15,12,13},{18,19,16,17},{22,23,20,2..., dimensions={0} | all-to-all | bytes 262144 | tf_op jit(solution)/shard_map/all_to_all | solution.py:412
  10.8 0.0 copy-done.2
  10.8 0.0 copy-done
  10.8 0.0 copy-done.1
  10.8 0.3 shard_map.74
  11.1 8.0 %all-gather = f32[16,2,6,8,128]{4,3,2,1,0:T(8,128)S(1)} all-gather(f32[8,2,6,8,128]{4,3,2,1,0:T(8,128)S(1)} %get-tuple-element.20), channel_id=2, replica_groups={{0,4},{8,12},{16,20},{24,28},{32,36},{40,44},{48,52},{56,60},{64,68},{7..., dimensions={0}, use_global_device_ids=true | all-gather | bytes 1179648 | tf_op jit(solution)/shard_map/all_gather | solution.py:445
  19.1 0.1 shard_map.75
  19.2 9.8 %all_to_all.21.received = f32[16,11,2,128]{3,2,1,0:T(2,128)S(1)} all-to-all(f32[16,11,2,128]{3,2,1,0:T(2,128)S(1)} %get-tuple-element.21), channel_id=1, replica_groups={{80,48,72,88,112,40,56,104,120,8,16,24,0,32,64,96},{84,52,76,92,116,44,..., dimensions={0} | all-to-all | bytes 360448 | tf_op jit(solution)/shard_map/all_to_all | solution.py:412
  28.9 0.1 shard_map.76
  29.0 13.9 %all_to_all.22.received = f32[4,24,128]{2,1,0:T(8,128)S(1)} all-to-all(f32[4,24,128]{2,1,0:T(8,128)S(1)} %get-tuple-element.22), channel_id=1, replica_groups={{256,384,0,128},{260,388,4,132},{264,392,8,136},{268,396,12,140},{272,4..., dimensions={0} | all-to-all | bytes 98304 | tf_op jit(solution)/shard_map/all_to_all | solution.py:412
  43.0 0.1 shard_map.77
  43.0 14.0 %all_to_all.23.received = f32[32,8,128]{2,1,0:T(8,128)S(1)} all-to-all(f32[32,8,128]{2,1,0:T(8,128)S(1)} %shard_map.77), channel_id=1, replica_groups={{84,88,92,96,100,104,108,112,116,120,124,0,4,8,12,16,20,24,28,32,36,40,..., dimensions={0} | all-to-all | bytes 262144 | tf_op jit(solution)/shard_map/all_to_all | solution.py:412
  57.0 1.1 %shard_map.78 = f32[256,256]{1,0:T(8,128)} custom-call(f32[32,8,128]{2,1,0:T(8,128)S(1)} %all_to_all.23.received, f32[8,2,3,8,128]{4,3,2,1,0:T(8,128)S(1)} %get-tuple-element.24.paired, f32[8,3,3,8,256]{4,3,2,1,0:T(8,128)S(1)} %get-tuple-element.25.kept, bf16[256,256]{1,0:T(8,128)(2,1)S(1)} %get-tuple-element.26.high, ...), custom_call_target="tpu_custom_call" | custom-call | tf_op jit(solution)/shard_map/pallas_call | solution.py:388
Async XLA Ops:
  0.0 10.8 %copy-start.2 = (f32[4,32,256]{2,1,0:T(8,128)S(1)}, f32[4,32,256]{2,1,0:T(8,128)}, u32[]{:S(2)}) copy-start(f32[4,32,256]{2,1,0:T(8,128)} %param.10) | copy-start | bytes 393220
  2.4 8.4 %copy-start = (f32[4,32,256]{2,1,0:T(8,128)S(1)}, f32[4,32,256]{2,1,0:T(8,128)}, u32[]{:S(2)}) copy-start(f32[4,32,256]{2,1,0:T(8,128)} %param.8) | copy-start | bytes 393220
  2.4 8.4 %copy-start.1 = (f32[4,32,256]{2,1,0:T(8,128)S(1)}, f32[4,32,256]{2,1,0:T(8,128)}, u32[]{:S(2)}) copy-start(f32[4,32,256]{2,1,0:T(8,128)} %param.9) | copy-start | bytes 393220
